TPU v7x, 32 devices: a whole 2x2x4 slice. The times are simulated.
32 devices in a mesh: dp: 8 (over y, x, core), mp: 4 (over z).
Axes of the slice: x: 2, y: 2, z: 4, core: 2. Of those that a mesh axis runs over, the one named last changes fastest.
Arguments:
- word_inputs: bfloat16 [8, 1024, 512], P('dp'), may hold values from -6 to 6
- character_embeddings: bfloat16 [160, 128, 16, 256], P('dp', 'mp'), may hold values from -6 to 6
- cotangent: bfloat16 [8, 1024, 512], P('dp'), may hold values from -6 to 6
- char_count: int32 [160, 128], P('dp', 'mp'), may hold values from 1 to 16, as said below
- word_place: int32 [160, 128], P('dp'), may hold values from -1 to 1023, as said below
- block_home: int32 [160], P('dp'), may hold values from -1 to 7, as said below
- documents: int32 [8, 1024], P('dp'), may hold values from 0 to 5, never falling along the last dimension, each value on 1 to 512 neighbouring positions
- char_gain: float32 [256], replicated, may hold values from 0.5 to 1.5
- word_gains: float32 [2, 512], replicated, may hold values from 0.5 to 1.5
- char_mixer: float32 [4, 256, 256], P(None, 'dp'), may hold values from -0.375 to 0.375
- char_mixer_left: float32 [4, 256, 256], P(None, 'dp'), as said below
- char_mixer_right: float32 [4, 256, 256], P(None, 'dp'), as said below
- char_mixer_left_root: float32 [4, 256, 256], P(None, 'dp'), as said below
- char_mixer_right_root: float32 [4, 256, 256], P(None, 'dp'), as said below
- char_lift: float32 [1, 256, 512], P(None, 'dp'), may hold values from -0.375 to 0.375
- char_lift_left: float32 [1, 256, 256], P(None, 'dp'), as said below
- char_lift_right: float32 [1, 512, 512], P(None, 'dp'), as said below
- char_lift_left_root: float32 [1, 256, 256], P(None, 'dp'), as said below
- char_lift_right_root: float32 [1, 512, 512], P(None, 'dp'), as said below
- word_project: float32 [3, 4, 512, 128], P(None, 'mp', 'dp'), may hold values from -0.25 to 0.25
- word_project_left: float32 [3, 4, 512, 512], P(None, 'mp', 'dp'), as said below
- word_project_right: float32 [3, 4, 128, 128], P(None, 'mp', 'dp'), as said below
- word_project_left_root: float32 [3, 4, 512, 512], P(None, 'mp', 'dp'), as said below
- word_project_right_root: float32 [3, 4, 128, 128], P(None, 'mp', 'dp'), as said below
- word_output: float32 [4, 128, 512], P('mp', 'dp'), may hold values from -1 to 1
- word_output_left: float32 [4, 128, 128], P('mp', 'dp'), as said below
- word_output_right: float32 [4, 512, 512], P('mp', 'dp'), as said below
- word_output_left_root: float32 [4, 128, 128], P('mp', 'dp'), as said below
- word_output_right_root: float32 [4, 512, 512], P('mp', 'dp'), as said below
- feed_upper: float32 [4, 512, 512], P('mp', 'dp'), may hold values from -0.25 to 0.25
- feed_upper_left: float32 [4, 512, 512], P('mp', 'dp'), as said below
- feed_upper_right: float32 [4, 512, 512], P('mp', 'dp'), as said below
- feed_upper_left_root: float32 [4, 512, 512], P('mp', 'dp'), as said below
- feed_upper_right_root: float32 [4, 512, 512], P('mp', 'dp'), as said below
- feed_lower: float32 [4, 512, 512], P('mp', 'dp'), may hold values from -0.125 to 0.125
- feed_lower_left: float32 [4, 512, 512], P('mp', 'dp'), as said below
- feed_lower_right: float32 [4, 512, 512], P('mp', 'dp'), as said below
- feed_lower_left_root: float32 [4, 512, 512], P('mp', 'dp'), as said below
- feed_lower_right_root: float32 [4, 512, 512], P('mp', 'dp'), as said below
Outputs:
- block_out: bfloat16 [8, 1024, 512], P('dp')
- word_inputs_gradient: bfloat16 [8, 1024, 512], P('dp')
- char_embeds_gradient: bfloat16 [160, 128, 16, 256], P('dp', 'mp')
- char_gain_gradient: float32 [256], replicated
- word_gains_gradient: float32 [2, 512], replicated
- char_gain_new: float32 [256], replicated
- word_gains_new: float32 [2, 512], replicated
- global_norm: float32 [], replicated
- char_mixer_gradient: float32 [4, 256, 256], P(None, 'dp')
- char_mixer_left_new: float32 [4, 256, 256], P(None, 'dp')
- char_mixer_right_new: float32 [4, 256, 256], P(None, 'dp')
- char_mixer_new: float32 [4, 256, 256], P(None, 'dp')
- char_mixer_copy: bfloat16 [4, 256, 256], P(None, 'dp')
- char_lift_gradient: float32 [1, 256, 512], P(None, 'dp')
- char_lift_left_new: float32 [1, 256, 256], P(None, 'dp')
- char_lift_right_new: float32 [1, 512, 512], P(None, 'dp')
- char_lift_new: float32 [1, 256, 512], P(None, 'dp')
- char_lift_copy: bfloat16 [1, 256, 512], P(None, 'dp')
- word_project_gradient: float32 [3, 4, 512, 128], P(None, 'mp', 'dp')
- word_project_left_new: float32 [3, 4, 512, 512], P(None, 'mp', 'dp')
- word_project_right_new: float32 [3, 4, 128, 128], P(None, 'mp', 'dp')
- word_project_new: float32 [3, 4, 512, 128], P(None, 'mp', 'dp')
- word_project_copy: bfloat16 [3, 4, 512, 128], P(None, 'mp', 'dp')
- word_output_gradient: float32 [4, 128, 512], P('mp', 'dp')
- word_output_left_new: float32 [4, 128, 128], P('mp', 'dp')
- word_output_right_new: float32 [4, 512, 512], P('mp', 'dp')
- word_output_new: float32 [4, 128, 512], P('mp', 'dp')
- word_output_copy: bfloat16 [4, 128, 512], P('mp', 'dp')
- feed_upper_gradient: float32 [4, 512, 512], P('mp', 'dp')
- feed_upper_left_new: float32 [4, 512, 512], P('mp', 'dp')
- feed_upper_right_new: float32 [4, 512, 512], P('mp', 'dp')
- feed_upper_new: float32 [4, 512, 512], P('mp', 'dp')
- feed_upper_copy: bfloat16 [4, 512, 512], P('mp', 'dp')
- feed_lower_gradient: float32 [4, 512, 512], P('mp', 'dp')
- feed_lower_left_new: float32 [4, 512, 512], P('mp', 'dp')
- feed_lower_right_new: float32 [4, 512, 512], P('mp', 'dp')
- feed_lower_new: float32 [4, 512, 512], P('mp', 'dp')
- feed_lower_copy: bfloat16 [4, 512, 512], P('mp', 'dp')
Inputs may be any that keep to these rules, and one draw needn't show every extreme that they name: Slots s of index i of dp are i * 20 to (i + 1) * 20 - 1; block_home names the owner of the block in a slot, -1 an empty slot; the live slots of an index come first. Each owner has exactly 10 blocks in all; no index holds more than 3 blocks of one owner, and some index does; some index has all 20 slots live. word_place is -1 on empty places and empty slots; over the slots of one owner each of its 1024 places appears exactly once. `char_count`: within one block all counts lie in one range (k - 1) * 4 + 1 to k * 4 for some k of 1 to 4. `char_mixer_left`: statistics of the previous step. `char_mixer_right`: statistics of the previous step. `char_mixer_left_root`: inverse roots of earlier statistics. `char_mixer_right_root`: inverse roots of earlier statistics. `char_lift_left`: statistics of the previous step. `char_lift_right`: statistics of the previous step. `char_lift_left_root`: inverse roots of earlier statistics. `char_lift_right_root`: inverse roots of earlier statistics. `word_project_left`: statistics of the previous step. `word_project_right`: statistics of the previous step. `word_project_left_root`: inverse roots of earlier statistics. `word_project_right_root`: inverse roots of earlier statistics. `word_output_left`: statistics of the previous step. `word_output_right`: statistics of the previous step. `word_output_left_root`: inverse roots of earlier statistics. `word_output_right_root`: inverse roots of earlier statistics. `feed_upper_left`: statistics of the previous step. `feed_upper_right`: statistics of the previous step. `feed_upper_left_root`: inverse roots of earlier statistics. `feed_upper_right_root`: inverse roots of earlier statistics. `feed_lower_left`: statistics of the previous step. `feed_lower_right`: statistics of the previous step. `feed_lower_left_root`: inverse roots of earlier statistics. `feed_lower_right_root`: inverse roots of earlier statistics.
All inputs are finite; a program needn't handle non-finite values.
Results may differ from a plain program's by a relative error of at most 0.024.
Values may be sent and summed in bfloat16 or wider, within the bound.
A program may use at most 256 MiB of HBM per device.

v0:
```python
import math

import jax
import jax.numpy as jnp
from jax import lax
from jax.sharding import PartitionSpec as P

D = 512
HD = 64
FF = 2048
CHAR_BLOCK_WIDTH = 256
CHEADS = 4
CHD = 64
WORD_CHAR_SPOTS = 16


epsilon = 1e-05
decay_rate = 0.5
learn_rate = 1.0
gain_rate = 0.4
highest = lax.Precision.HIGHEST
negative_big = -1e30


def norm_forward(values, gain_row):
    row_scale = lax.rsqrt(jnp.mean(values * values, axis=-1, keepdims=True) + epsilon)
    return (values * row_scale * gain_row, row_scale)


def norm_backward(values, row_scale, gain_row, grad_output):
    weighted = grad_output * gain_row
    row_inner = jnp.mean(values * weighted, axis=-1, keepdims=True)
    grad_values = row_scale * weighted - values * (row_scale * row_scale * row_scale) * row_inner
    return (grad_values, jnp.sum(values * row_scale * grad_output, axis=0))


def gelu_tanh(values):
    return jax.nn.gelu(values, approximate=True)


def char_softmax(queries, keys_all, visible):
    scores = jnp.einsum(
        "wqhe,wkhe->whqk", queries, keys_all, preferred_element_type=jnp.float32
    ) / math.sqrt(CHD)
    return jax.nn.softmax(jnp.where(visible[:, None, None, :], scores, negative_big), axis=-1)


def char_forward(char_rows, counts, char_gain, mixer_mats, lift_mats):
    word_count = char_rows.shape[0] * char_rows.shape[1]
    flat_chars = char_rows.reshape(word_count * WORD_CHAR_SPOTS, CHAR_BLOCK_WIDTH)
    normed_float, row_scale = norm_forward(flat_chars.astype(jnp.float32), char_gain)
    normed = normed_float.astype(jnp.bfloat16)
    projected = jnp.einsum(
        "rd,tde->tre", normed, mixer_mats[:3], preferred_element_type=jnp.float32
    ).astype(jnp.bfloat16)
    heads_view = projected.reshape(3, word_count, WORD_CHAR_SPOTS, CHEADS, CHD)
    visible = lax.broadcasted_iota(jnp.int32, (word_count, WORD_CHAR_SPOTS), 1) < counts.reshape(
        word_count, 1
    )
    attention = char_softmax(heads_view[0], heads_view[1], visible).astype(jnp.bfloat16)
    mixed_rows = jnp.einsum(
        "whqk,wkhe->wqhe", attention, heads_view[2], preferred_element_type=jnp.float32
    )
    mixed_rows = mixed_rows.astype(jnp.bfloat16).reshape(
        word_count * WORD_CHAR_SPOTS, CHAR_BLOCK_WIDTH
    )
    summed = flat_chars.astype(jnp.float32) + jnp.dot(
        mixed_rows, mixer_mats[3], preferred_element_type=jnp.float32
    )
    pooled_sum = jnp.sum(
        jnp.where(
            visible[:, :, None], summed.reshape(word_count, WORD_CHAR_SPOTS, CHAR_BLOCK_WIDTH), 0.0
        ),
        axis=1,
    )
    count_float = counts.reshape(word_count, 1).astype(jnp.float32)
    pooled = (pooled_sum / count_float).astype(jnp.bfloat16)
    word_vectors = jnp.dot(pooled, lift_mats[0], preferred_element_type=jnp.float32).astype(
        jnp.bfloat16
    )
    return (
        word_vectors,
        (flat_chars, row_scale, normed, projected, mixed_rows, pooled, visible, count_float),
    )


def char_backward(char_rows, char_gain, mixer_mats, lift_mats, kept_values, grad_vectors):
    flat_chars, row_scale, normed, projected, mixed_rows, pooled, visible, count_float = kept_values
    word_count = pooled.shape[0]
    grad_lift = jnp.einsum("wd,we->de", pooled, grad_vectors, preferred_element_type=jnp.float32)
    grad_pooled = (
        jnp.einsum("we,de->wd", grad_vectors, lift_mats[0], preferred_element_type=jnp.float32)
        / count_float
    )
    grad_summed = jnp.where(visible[:, :, None], grad_pooled[:, None, :], 0.0).reshape(
        word_count * WORD_CHAR_SPOTS, CHAR_BLOCK_WIDTH
    )
    grad_branch = grad_summed.astype(jnp.bfloat16)
    grad_out_mat = jnp.einsum(
        "rd,re->de", mixed_rows, grad_branch, preferred_element_type=jnp.float32
    )
    grad_mixed = jnp.einsum(
        "re,de->rd", grad_branch, mixer_mats[3], preferred_element_type=jnp.float32
    )
    grad_mixed = grad_mixed.astype(jnp.bfloat16).reshape(word_count, WORD_CHAR_SPOTS, CHEADS, CHD)
    heads_view = projected.reshape(3, word_count, WORD_CHAR_SPOTS, CHEADS, CHD)
    attention = char_softmax(heads_view[0], heads_view[1], visible)
    grad_attention = jnp.einsum(
        "wqhe,wkhe->whqk", grad_mixed, heads_view[2], preferred_element_type=jnp.float32
    )
    row_inner = jnp.sum(attention * grad_attention, axis=-1, keepdims=True)
    grad_scores = (attention * (grad_attention - row_inner)).astype(jnp.bfloat16)
    root_size = math.sqrt(CHD)
    grad_queries = (
        jnp.einsum(
            "whqk,wkhe->wqhe", grad_scores, heads_view[1], preferred_element_type=jnp.float32
        )
        / root_size
    )
    grad_keys = (
        jnp.einsum(
            "whqk,wqhe->wkhe", grad_scores, heads_view[0], preferred_element_type=jnp.float32
        )
        / root_size
    )
    grad_values = jnp.einsum(
        "whqk,wqhe->wkhe",
        attention.astype(jnp.bfloat16),
        grad_mixed,
        preferred_element_type=jnp.float32,
    )
    grad_heads = (
        jnp.stack([grad_queries, grad_keys, grad_values])
        .astype(jnp.bfloat16)
        .reshape(3, word_count * WORD_CHAR_SPOTS, CHAR_BLOCK_WIDTH)
    )
    grad_in_mats = jnp.einsum("rd,tre->tde", normed, grad_heads, preferred_element_type=jnp.float32)
    grad_normed = jnp.einsum(
        "tre,tde->rd", grad_heads, mixer_mats[:3], preferred_element_type=jnp.float32
    )
    grad_from_norm, grad_gain = norm_backward(
        flat_chars.astype(jnp.float32), row_scale, char_gain, grad_normed
    )
    grad_chars = (grad_summed + grad_from_norm).astype(jnp.bfloat16).reshape(char_rows.shape)
    grad_mixer = jnp.concatenate([grad_in_mats, grad_out_mat[None]], axis=0)
    return (grad_chars, grad_mixer, grad_lift[None], grad_gain)


def word_softmax(row_queries, row_keys, query_docs, key_docs, first_row):
    scores = jnp.einsum(
        "qhe,khe->hqk", row_queries, row_keys, preferred_element_type=jnp.float32
    ) / math.sqrt(HD)
    table_shape = (row_queries.shape[0], row_keys.shape[0])
    query_at = first_row + lax.broadcasted_iota(jnp.int32, table_shape, 0)
    key_at = lax.broadcasted_iota(jnp.int32, table_shape, 1)
    allowed = (key_at <= query_at) & (key_docs[None, :] == query_docs[:, None])
    return jax.nn.softmax(jnp.where(allowed[None], scores, negative_big), axis=-1)


def word_attention(queries, keys_all, values_all, documents):
    length = queries.shape[1]
    block_rows = min(512, length)

    def one_row(pieces):
        row_queries, row_keys, row_values, row_docs = pieces
        outputs = []
        for first_row in range(0, length, block_rows):
            last_row = first_row + block_rows
            attention = word_softmax(
                row_queries[first_row:last_row],
                row_keys,
                row_docs[first_row:last_row],
                row_docs,
                first_row,
            )
            outputs.append(
                jnp.einsum(
                    "hqk,khe->qhe",
                    attention.astype(jnp.bfloat16),
                    row_values,
                    preferred_element_type=jnp.float32,
                ).astype(jnp.bfloat16)
            )
        return jnp.concatenate(outputs, axis=0)

    return lax.map(one_row, (queries, keys_all, values_all, documents))


def word_attention_back(queries, keys_all, values_all, grad_mixed, documents):
    length = queries.shape[1]
    block_rows = min(512, length)
    root_size = math.sqrt(HD)

    def one_row(pieces):
        row_queries, row_keys, row_values, row_grads, row_docs = pieces
        query_parts = []
        grad_keys = jnp.zeros(row_keys.shape, jnp.float32)
        grad_values = jnp.zeros(row_values.shape, jnp.float32)
        for first_row in range(0, length, block_rows):
            last_row = first_row + block_rows
            attention = word_softmax(
                row_queries[first_row:last_row],
                row_keys,
                row_docs[first_row:last_row],
                row_docs,
                first_row,
            )
            grad_attention = jnp.einsum(
                "qhe,khe->hqk",
                row_grads[first_row:last_row],
                row_values,
                preferred_element_type=jnp.float32,
            )
            row_inner = jnp.sum(attention * grad_attention, axis=-1, keepdims=True)
            grad_scores = (attention * (grad_attention - row_inner)).astype(jnp.bfloat16)
            query_parts.append(
                jnp.einsum(
                    "hqk,khe->qhe", grad_scores, row_keys, preferred_element_type=jnp.float32
                )
                / root_size
            )
            grad_keys = (
                grad_keys
                + jnp.einsum(
                    "hqk,qhe->khe",
                    grad_scores,
                    row_queries[first_row:last_row],
                    preferred_element_type=jnp.float32,
                )
                / root_size
            )
            grad_values = grad_values + jnp.einsum(
                "hqk,qhe->khe",
                attention.astype(jnp.bfloat16),
                row_grads[first_row:last_row],
                preferred_element_type=jnp.float32,
            )
        grad_queries = jnp.concatenate(query_parts, axis=0)
        return (
            grad_queries.astype(jnp.bfloat16),
            grad_keys.astype(jnp.bfloat16),
            grad_values.astype(jnp.bfloat16),
        )

    return lax.map(one_row, (queries, keys_all, values_all, grad_mixed, documents))


def refresh(master, gradient, left_stat, right_stat, left_root, right_root, factor, owner_index):
    clipped = gradient * factor
    rows_own = master.shape[-2]
    cols_own = right_stat.shape[-2]
    own_rows = lax.dynamic_slice_in_dim(clipped, owner_index * rows_own, rows_own, clipped.ndim - 2)
    own_cols = lax.dynamic_slice_in_dim(clipped, owner_index * cols_own, cols_own, clipped.ndim - 1)
    left_new = decay_rate * left_stat + (1.0 - decay_rate) * jnp.einsum(
        "...mn,...kn->...mk", own_rows, clipped, precision=highest
    )
    right_new = decay_rate * right_stat + (1.0 - decay_rate) * jnp.einsum(
        "...mn,...mk->...nk", own_cols, clipped, precision=highest
    )
    shampoo_step = jnp.matmul(
        jnp.matmul(left_root, clipped, precision=highest), right_root, precision=highest
    )
    fresh_master = master - learn_rate * shampoo_step
    return (own_rows, left_new, right_new, fresh_master, fresh_master.astype(jnp.bfloat16))


def local(
    word_inputs,
    character_embeddings,
    cotangent,
    char_count,
    word_place,
    block_home,
    documents,
    char_gain,
    word_gains,
    char_mixer,
    char_mixer_left,
    char_mixer_right,
    char_mixer_left_root,
    char_mixer_right_root,
    char_lift,
    char_lift_left,
    char_lift_right,
    char_lift_left_root,
    char_lift_right_root,
    word_project,
    word_project_left,
    word_project_right,
    word_project_left_root,
    word_project_right_root,
    word_output,
    word_output_left,
    word_output_right,
    word_output_left_root,
    word_output_right_root,
    feed_upper,
    feed_upper_left,
    feed_upper_right,
    feed_upper_left_root,
    feed_upper_right_root,
    feed_lower,
    feed_lower_left,
    feed_lower_right,
    feed_lower_left_root,
    feed_lower_right_root,
):
    mixer_mats, lift_mats, project_mats, output_mats, upper_mats, lower_mats = (
        lax.all_gather(char_mixer.astype(jnp.bfloat16), "dp", axis=1, tiled=True),
        lax.all_gather(char_lift.astype(jnp.bfloat16), "dp", axis=1, tiled=True),
        lax.all_gather(word_project.astype(jnp.bfloat16), "dp", axis=2, tiled=True),
        lax.all_gather(word_output.astype(jnp.bfloat16), "dp", axis=1, tiled=True),
        lax.all_gather(feed_upper.astype(jnp.bfloat16), "dp", axis=1, tiled=True),
        lax.all_gather(feed_lower.astype(jnp.bfloat16), "dp", axis=1, tiled=True),
    )
    slot_count, share_rows = (character_embeddings.shape[0], character_embeddings.shape[1])
    word_vectors, kept_chars = char_forward(
        character_embeddings, char_count, char_gain, mixer_mats, lift_mats
    )
    peer_count = lax.axis_size("dp")
    pair_cap = -(-slot_count // peer_count)
    slot_total = peer_count * pair_cap
    owner_match = (
        block_home[:, None] == lax.broadcasted_iota(jnp.int32, (slot_count, peer_count), 1)
    ).astype(jnp.int32)
    slot_rank = jnp.sum((jnp.cumsum(owner_match, axis=0) - owner_match) * owner_match, axis=1)
    slot_target = jnp.where(block_home >= 0, block_home * pair_cap + slot_rank, slot_total)
    lane_start = lax.axis_index("mp") * share_rows
    rows_dev, length = (word_inputs.shape[0], word_inputs.shape[1])
    words_dev = rows_dev * length

    def place_slots(values, fill_value):
        buffer = jnp.full((slot_total,) + values.shape[1:], fill_value, values.dtype)
        return buffer.at[slot_target].set(values, mode="drop")

    vector_blocks = word_vectors.reshape(slot_count, share_rows, D)
    whole_vectors = lax.all_gather(vector_blocks, "mp", axis=1, tiled=True)
    came_vectors, came_place = (
        lax.all_to_all(
            place_slots(whole_vectors, 0), "dp", split_axis=0, concat_axis=0, tiled=True
        ),
        lax.all_to_all(place_slots(word_place, -1), "dp", split_axis=0, concat_axis=0, tiled=True),
    )
    flat_place = came_place.reshape(-1)
    placed = (
        jnp.zeros((words_dev, D), jnp.float32)
        .at[jnp.where(flat_place >= 0, flat_place, words_dev)]
        .set(came_vectors.reshape(-1, D).astype(jnp.float32), mode="drop")
    )
    stream = word_inputs.reshape(words_dev, D).astype(jnp.float32) + placed
    normed_float, scale_one = norm_forward(stream, word_gains[0])
    normed_one = normed_float.astype(jnp.bfloat16)
    block_width = output_mats.shape[1]
    local_heads = block_width // HD
    projected = jnp.einsum(
        "rd,tde->tre", normed_one, project_mats[:, 0], preferred_element_type=jnp.float32
    ).astype(jnp.bfloat16)
    heads_view = projected.reshape(3, rows_dev, length, local_heads, HD)
    mixed_rows = word_attention(heads_view[0], heads_view[1], heads_view[2], documents).reshape(
        words_dev, block_width
    )
    attend_total = lax.psum(
        jnp.dot(mixed_rows, output_mats[0], preferred_element_type=jnp.float32).astype(
            jnp.bfloat16
        ),
        "mp",
    ).astype(jnp.float32)
    hidden = stream + attend_total
    normed_float_two, scale_two = norm_forward(hidden, word_gains[1])
    normed_two = normed_float_two.astype(jnp.bfloat16)
    upper_rows = jnp.dot(normed_two, upper_mats[0], preferred_element_type=jnp.float32)
    active = gelu_tanh(upper_rows).astype(jnp.bfloat16)
    feed_total = lax.psum(
        jnp.dot(active, lower_mats[0], preferred_element_type=jnp.float32).astype(jnp.bfloat16),
        "mp",
    ).astype(jnp.float32)
    block_out = (hidden + feed_total).astype(jnp.bfloat16).reshape(word_inputs.shape)
    grad_output = cotangent.reshape(words_dev, D).astype(jnp.float32)
    grad_feed = grad_output.astype(jnp.bfloat16)
    grad_lower = jnp.einsum("rf,rd->fd", active, grad_feed, preferred_element_type=jnp.float32)
    grad_active = jnp.einsum(
        "rd,fd->rf", grad_feed, lower_mats[0], preferred_element_type=jnp.float32
    )
    unused_value, gelu_pull = jax.vjp(gelu_tanh, upper_rows)
    grad_upper_rows = gelu_pull(grad_active)[0].astype(jnp.bfloat16)
    grad_upper = jnp.einsum(
        "rd,rf->df", normed_two, grad_upper_rows, preferred_element_type=jnp.float32
    )
    part_two = jnp.einsum(
        "rf,df->rd", grad_upper_rows, upper_mats[0], preferred_element_type=jnp.float32
    )
    grad_normed_two = lax.psum(part_two.astype(jnp.bfloat16), "mp").astype(jnp.float32)
    grad_hidden_norm, gain_two = norm_backward(hidden, scale_two, word_gains[1], grad_normed_two)
    grad_hidden = grad_output + grad_hidden_norm
    grad_attend = grad_hidden.astype(jnp.bfloat16)
    grad_output_mat = jnp.einsum(
        "re,rd->ed", mixed_rows, grad_attend, preferred_element_type=jnp.float32
    )
    grad_mixed = jnp.einsum(
        "rd,ed->re", grad_attend, output_mats[0], preferred_element_type=jnp.float32
    ).astype(jnp.bfloat16)
    grad_queries, grad_keys, grad_values = word_attention_back(
        heads_view[0],
        heads_view[1],
        heads_view[2],
        grad_mixed.reshape(rows_dev, length, local_heads, HD),
        documents,
    )
    grad_heads = jnp.stack([grad_queries, grad_keys, grad_values]).reshape(
        3, words_dev, block_width
    )
    grad_project = jnp.einsum(
        "rd,tre->tde", normed_one, grad_heads, preferred_element_type=jnp.float32
    )
    part_one = jnp.einsum(
        "tre,tde->rd", grad_heads, project_mats[:, 0], preferred_element_type=jnp.float32
    )
    grad_normed_one = lax.psum(part_one.astype(jnp.bfloat16), "mp").astype(jnp.float32)
    grad_stream_norm, gain_one = norm_backward(stream, scale_one, word_gains[0], grad_normed_one)
    grad_stream = grad_hidden + grad_stream_norm
    word_inputs_gradient = grad_stream.astype(jnp.bfloat16).reshape(word_inputs.shape)
    grad_words = grad_stream.astype(jnp.bfloat16)
    picked = jnp.where(came_place[..., None] >= 0, grad_words[jnp.maximum(came_place, 0)], 0.0)
    returned = lax.all_to_all(picked, "dp", split_axis=0, concat_axis=0, tiled=True)
    own_vectors = lax.dynamic_slice_in_dim(returned, lane_start, share_rows, 1)
    grad_vectors = jnp.where(
        (block_home >= 0)[:, None, None], own_vectors[jnp.minimum(slot_target, slot_total - 1)], 0.0
    )
    grad_vectors = grad_vectors.reshape(slot_count * share_rows, D)
    char_embeds_gradient, grad_mixer, grad_lift, grad_char_gain = char_backward(
        character_embeddings, char_gain, mixer_mats, lift_mats, kept_chars, grad_vectors
    )
    sum_project, sum_output, sum_upper, sum_lower, sum_word_gains = (
        lax.psum(grad_project[:, None].astype(jnp.bfloat16), "dp").astype(jnp.float32),
        lax.psum(grad_output_mat[None].astype(jnp.bfloat16), "dp").astype(jnp.float32),
        lax.psum(grad_upper[None].astype(jnp.bfloat16), "dp").astype(jnp.float32),
        lax.psum(grad_lower[None].astype(jnp.bfloat16), "dp").astype(jnp.float32),
        lax.psum(jnp.stack([gain_one, gain_two]).astype(jnp.bfloat16), "dp").astype(jnp.float32),
    )
    word_squares = (
        jnp.sum(sum_project * sum_project)
        + jnp.sum(sum_output * sum_output)
        + jnp.sum(sum_upper * sum_upper)
        + jnp.sum(sum_lower * sum_lower)
    )
    sum_mixer, sum_lift, sum_char_gain, spread_squares = lax.psum(
        (grad_mixer, grad_lift, grad_char_gain, word_squares), ("dp", "mp")
    )
    other_squares = (
        jnp.sum(sum_mixer * sum_mixer)
        + jnp.sum(sum_lift * sum_lift)
        + jnp.sum(sum_char_gain * sum_char_gain)
        + jnp.sum(sum_word_gains * sum_word_gains)
    )
    global_norm = jnp.sqrt(spread_squares / float(peer_count) + other_squares)
    threshold = 0.5 * math.sqrt(
        4 * CHAR_BLOCK_WIDTH * CHAR_BLOCK_WIDTH
        + CHAR_BLOCK_WIDTH * D
        + 4 * D * D
        + 2 * D * FF
        + CHAR_BLOCK_WIDTH
        + 2 * D
    )
    factor = jnp.minimum(1.0, threshold / global_norm)
    owner_index = lax.axis_index("dp")
    mixer_root, lift_root, project_root, output_root, upper_root, lower_root = (
        lax.all_gather(char_mixer_right_root.astype(jnp.bfloat16), "dp", axis=1, tiled=True).astype(
            char_mixer_right_root.dtype
        ),
        lax.all_gather(char_lift_right_root.astype(jnp.bfloat16), "dp", axis=1, tiled=True).astype(
            char_lift_right_root.dtype
        ),
        lax.all_gather(
            word_project_right_root.astype(jnp.bfloat16), "dp", axis=2, tiled=True
        ).astype(word_project_right_root.dtype),
        lax.all_gather(
            word_output_right_root.astype(jnp.bfloat16), "dp", axis=1, tiled=True
        ).astype(word_output_right_root.dtype),
        lax.all_gather(feed_upper_right_root.astype(jnp.bfloat16), "dp", axis=1, tiled=True).astype(
            feed_upper_right_root.dtype
        ),
        lax.all_gather(feed_lower_right_root.astype(jnp.bfloat16), "dp", axis=1, tiled=True).astype(
            feed_lower_right_root.dtype
        ),
    )
    mixer_out = refresh(
        char_mixer,
        sum_mixer,
        char_mixer_left,
        char_mixer_right,
        char_mixer_left_root,
        mixer_root,
        factor,
        owner_index,
    )
    lift_out = refresh(
        char_lift,
        sum_lift,
        char_lift_left,
        char_lift_right,
        char_lift_left_root,
        lift_root,
        factor,
        owner_index,
    )
    project_out = refresh(
        word_project,
        sum_project,
        word_project_left,
        word_project_right,
        word_project_left_root,
        project_root,
        factor,
        owner_index,
    )
    output_out = refresh(
        word_output,
        sum_output,
        word_output_left,
        word_output_right,
        word_output_left_root,
        output_root,
        factor,
        owner_index,
    )
    upper_out = refresh(
        feed_upper,
        sum_upper,
        feed_upper_left,
        feed_upper_right,
        feed_upper_left_root,
        upper_root,
        factor,
        owner_index,
    )
    lower_out = refresh(
        feed_lower,
        sum_lower,
        feed_lower_left,
        feed_lower_right,
        feed_lower_left_root,
        lower_root,
        factor,
        owner_index,
    )
    char_gain_clipped = factor * sum_char_gain
    word_gains_clipped = factor * sum_word_gains
    return (
        block_out,
        word_inputs_gradient,
        char_embeds_gradient,
        char_gain_clipped,
        word_gains_clipped,
        char_gain - gain_rate * char_gain_clipped,
        word_gains - gain_rate * word_gains_clipped,
        global_norm,
        mixer_out[0],
        mixer_out[1],
        mixer_out[2],
        mixer_out[3],
        mixer_out[4],
        lift_out[0],
        lift_out[1],
        lift_out[2],
        lift_out[3],
        lift_out[4],
        project_out[0],
        project_out[1],
        project_out[2],
        project_out[3],
        project_out[4],
        output_out[0],
        output_out[1],
        output_out[2],
        output_out[3],
        output_out[4],
        upper_out[0],
        upper_out[1],
        upper_out[2],
        upper_out[3],
        upper_out[4],
        lower_out[0],
        lower_out[1],
        lower_out[2],
        lower_out[3],
        lower_out[4],
    )


def solution(mesh):
    placed = (
        P("dp", None, None),
        P("dp", "mp", None, None),
        P("dp", None, None),
        P("dp", "mp"),
        P("dp", None),
        P("dp"),
        P("dp", None),
        P(),
        P(),
        P(None, "dp", None),
        P(None, "dp", None),
        P(None, "dp", None),
        P(None, "dp", None),
        P(None, "dp", None),
        P(None, "dp", None),
        P(None, "dp", None),
        P(None, "dp", None),
        P(None, "dp", None),
        P(None, "dp", None),
        P(None, "mp", "dp", None),
        P(None, "mp", "dp", None),
        P(None, "mp", "dp", None),
        P(None, "mp", "dp", None),
        P(None, "mp", "dp", None),
        P("mp", "dp", None),
        P("mp", "dp", None),
        P("mp", "dp", None),
        P("mp", "dp", None),
        P("mp", "dp", None),
        P("mp", "dp", None),
        P("mp", "dp", None),
        P("mp", "dp", None),
        P("mp", "dp", None),
        P("mp", "dp", None),
        P("mp", "dp", None),
        P("mp", "dp", None),
        P("mp", "dp", None),
        P("mp", "dp", None),
        P("mp", "dp", None),
    )
    return jax.shard_map(
        local,
        mesh=mesh,
        in_specs=placed,
        out_specs=(
            P("dp", None, None),
            P("dp", None, None),
            P("dp", "mp", None, None),
            P(),
            P(),
            P(),
            P(),
            P(),
            P(None, "dp", None),
            P(None, "dp", None),
            P(None, "dp", None),
            P(None, "dp", None),
            P(None, "dp", None),
            P(None, "dp", None),
            P(None, "dp", None),
            P(None, "dp", None),
            P(None, "dp", None),
            P(None, "dp", None),
            P(None, "mp", "dp", None),
            P(None, "mp", "dp", None),
            P(None, "mp", "dp", None),
            P(None, "mp", "dp", None),
            P(None, "mp", "dp", None),
            P("mp", "dp", None),
            P("mp", "dp", None),
            P("mp", "dp", None),
            P("mp", "dp", None),
            P("mp", "dp", None),
            P("mp", "dp", None),
            P("mp", "dp", None),
            P("mp", "dp", None),
            P("mp", "dp", None),
            P("mp", "dp", None),
            P("mp", "dp", None),
            P("mp", "dp", None),
            P("mp", "dp", None),
            P("mp", "dp", None),
            P("mp", "dp", None),
        ),
        check_vma=False,
    )
```

profile of v0, /device:TPU:0, one launch (start us, length us, event | category | flops | bytes accessed | tf_op | source)
XLA Modules:
  0.0 1141.0 jit_solution(5664233220624832067)
XLA Ops:
  65.1 16.0 %squeeze.104 = bf16[640,16,4,64]{3,2,1,0:T(4,128)(2,1)} reshape(bf16[1,10240,256]{2,1,0:T(8,128)(2,1)} %get-tuple-element.223) | data formatting | bytes 10485760 | tf_op jit(solution)/shard_map/squeeze | solution.py:60
  81.0 16.0 %squeeze.105 = bf16[640,16,4,64]{3,2,1,0:T(4,128)(2,1)} reshape(bf16[1,10240,256]{2,1,0:T(8,128)(2,1)} %get-tuple-element.224) | data formatting | bytes 10485760 | tf_op jit(solution)/shard_map/squeeze | solution.py:60
  97.0 16.0 %squeeze.103 = bf16[640,16,4,64]{3,2,1,0:T(4,128)(2,1)} reshape(bf16[1,10240,256]{2,1,0:T(8,128)(2,1)} %get-tuple-element.225) | data formatting | bytes 10485760 | tf_op jit(solution)/shard_map/squeeze | solution.py:62
  126.9 28.5 %fusion.240 = (f32[640,4,16]{2,1,0:T(4,128)S(1)}, f32[640,4,16,16]{2,3,1,0:T(8,128)}) fusion(f32[640,4,16,16]{2,3,1,0:T(8,128)} %fusion.29, pred[640,16]{1,0:T(8,128)(4,1)S(1)} %iota_compare_fusion.2), kind=kOutput, calls=%fused_computation.377 | output fusion | flops 3932175 | bytes 5416960 | tf_op jit(solution)/shard_map/sub | solution.py:45
  155.5 16.5 %convert_bitcast_fusion.1 = bf16[640,16,4,64]{3,1,2,0:T(8,128)(2,1)} fusion(bf16[640,16,4,64]{3,2,1,0:T(4,128)(2,1)} %squeeze.103, f32[640,4,16,16]{2,3,1,0:T(8,128)} %get-tuple-element.243, f32[640,4,16]{2,1,0:T(4,128)S(1)} %get-tuple-element.242), kind=kOutput, calls=%fused_computation.40 | convolution fusion | flops 87818240 | bytes 13271040 | tf_op jit(solution)/shard_map/whqk,wkhe->wqhe/dot_general | solution.py:61
  181.9 15.7 %reshape.618 = bf16[10240,256]{1,0:T(8,128)(2,1)} reshape(bf16[640,16,4,64]{3,2,1,0:T(4,128)(2,1)} %copy.154) | data formatting | bytes 10485760 | tf_op jit(solution)/shard_map/reshape | solution.py:64
  224.7 49.6 %all-gather.2.cloned.1.call-done = bf16[20,128,512]{2,1,0:T(8,128)(2,1)} async-done(((bf16[20,32,512]{2,1,0:T(8,128)(2,1)}), bf16[20,128,512]{2,1,0:T(8,128)(2,1)}) %all-gather.2.cloned.1.call-update) | async-done | bytes 2621456 | tf_op jit(solution)/shard_map/all_gather | solution.py:337
  290.4 40.4 %all_gather.42 = bf16[3,1,512,128]{3,2,1,0:T(8,128)(2,1)} all-gather(bf16[3,1,64,128]{3,2,1,0:T(8,128)(2,1)S(1)} %convert_element_type.330), channel_id=1, replica_groups=mesh['dp'=8,'mp'=4] {'dp'}, dimensions={2}, use_global_device_ids=true | all-gather | bytes 442368 | tf_op jit(solution)/shard_map/all_gather | solution.py:311
  349.2 15.1 %scatter_custom_fusion.2 = f32[1024,512]{1,0:T(8,128)} fusion(s32[3072]{0:T(1024)} %bitcast.465, bf16[3072,512]{1,0:T(8,128)(2,1)S(1)} %bitcast.424, f32[]{:T(128)} %constant.53.clone.1), kind=kCustom, calls=%fused_computation.59 | custom fusion | flops 1572864 | bytes 5243392 | tf_op jit(solution)/shard_map/scatter | solution.py:348
  402.6 29.9 %all-reduce.10.cloned.1.call-done = bf16[1024,512]{1,0:T(8,128)(2,1)} async-done(((bf16[1024,512]{1,0:T(8,128)(2,1)}), bf16[1024,512]{1,0:T(8,128)(2,1)}) %all-reduce.10.cloned.1.call-update) | async-done | bytes 1048592 | tf_op jit(solution)/shard_map/psum | solution.py:362
  443.8 47.8 %all-reduce.12.cloned.1.call-done = bf16[1024,512]{1,0:T(8,128)(2,1)} async-done(((bf16[1024,512]{1,0:T(8,128)(2,1)}), bf16[1024,512]{1,0:T(8,128)(2,1)}) %all-reduce.12.cloned.1.call-update) | async-done | bytes 1048592 | tf_op jit(solution)/shard_map/psum | solution.py:392
  571.2 36.8 %all-reduce.18.cloned.1.call-done = (bf16[1024,512]{1,0:T(8,128)(2,1)}, bf16[1024,512]{1,0:T(8,128)(2,1)}) async-done(((bf16[1024,512]{1,0:T(8,128)(2,1)}, bf16[1024,512]{1,0:T(8,128)(2,1)}), (bf16[1024,512]{1,0:T(8,128)(2,1)}, bf16[1024,512]{1,0:T(8,128)(2,1)})) %all-reduce.18.cloned.1.call-update) | async-done | bytes 2097168 | tf_op jit(solution)/shard_map/psum | solution.py:373
  642.1 43.4 %all_gather.47 = bf16[1,512,512]{2,1,0:T(8,128)(2,1)} all-gather(bf16[1,64,512]{2,1,0:T(8,128)(2,1)} %convert_element_type.385), channel_id=1, replica_groups=mesh['dp'=8,'mp'=4] {'dp'}, dimensions={1}, use_global_device_ids=true | all-gather | bytes 589824 | tf_op jit(solution)/shard_map/all_gather | solution.py:470
  698.7 15.4 %all-reduce.16.cloned.1.call-done = (bf16[3,1,512,128]{2,3,0,1:T(8,128)(2,1)}, bf16[1,128,512]{2,1,0:T(8,128)(2,1)}, bf16[1,512,512]{2,1,0:T(8,128)(2,1)}, bf16[1,512,512]{2,1,0:T(8,128)(2,1)}) async-done(((bf16[3,1,512,128]{2,3,0,1:T(8,128)(2,1)}, bf16[1,128,512]{2,1,0:T(8,128)(2,1)}, bf16[1,512,512]{2,1,0:T(8,128)(2,1)}, bf16[1,512,512]{2,1,0:T(8,128)(2,1)}), (bf16[3,1,512,128]{2,3,0,1:T(8,128)(2,1)}, ...) | async-done | bytes 1572880 | tf_op jit(solution)/shard_map/psum | solution.py:434
  751.1 16.1 %reshape.625 = bf16[640,16,4,64]{3,2,1,0:T(4,128)(2,1)} reshape(bf16[10240,256]{1,0:T(8,128)(2,1)} %convolution_convert_fusion.1) | data formatting | bytes 10485760 | tf_op jit(solution)/shard_map/reshape | solution.py:105
  767.1 16.6 %convert_bitcast_fusion = bf16[640,16,4,64]{3,1,2,0:T(8,128)(2,1)} fusion(bf16[640,16,4,64]{3,2,1,0:T(4,128)(2,1)} %reshape.625, f32[640,4,16,16]{2,3,1,0:T(8,128)} %get-tuple-element.243, f32[640,4,16]{2,1,0:T(4,128)S(1)} %copy-done.35), kind=kOutput, calls=%fused_computation.37 | convolution fusion | flops 87818240 | bytes 13271040 | tf_op jit(solution)/shard_map/whqk,wqhe->wkhe/dot_general | solution.py:126
  783.7 21.6 %multiply_reduce_fusion = (f32[640,4,16]{2,1,0:T(4,128)S(1)}, f32[640,4,16,16]{2,3,1,0:T(8,128)}) fusion(f32[640,4,16,16]{2,3,1,0:T(8,128)} %get-tuple-element.243, f32[640,4,16]{2,1,0:T(4,128)S(1)} %copy-done.35, bf16[640,16,4,64]{3,2,1,0:T(4,128)(2,1)} %squeeze.103, bf16[640,16,4,64]{3,2,1,0:T(4,128)(2,1)} %reshape.625), kind=kOutput, calls=%fused_computation.11 | convolution fusion | flops 85811200 | bytes 16056320 | tf_op jit(solution)/shard_map/wqhe,wkhe->whqk/dot_general | solution.py:108
  805.3 19.3 %multiply_convert_fusion.2 = bf16[640,4,16,16]{2,3,1,0:T(8,128)(2,1)} fusion(f32[640,4,16,16]{2,3,1,0:T(8,128)} %get-tuple-element.253, f32[640,4,16]{2,1,0:T(4,128)S(1)} %get-tuple-element.252, f32[640,4,16,16]{2,3,1,0:T(8,128)} %get-tuple-element.243, f32[640,4,16]{2,1,0:T(4,128)S(1)} %copy-done.35), kind=kLoop, calls=%fused_computation.10 | loop fusion | flops 2621440 | bytes 6881280 | tf_op jit(solution)/shard_map/convert_element_type | solution.py:112
  837.2 14.0 %fusion.5 = bf16[640,16,4,64]{3,1,2,0:T(8,128)(2,1)} fusion(bf16[640,4,16,16]{2,3,1,0:T(8,128)(2,1)} %multiply_convert_fusion.2, bf16[640,16,4,64]{3,2,1,0:T(4,128)(2,1)} %squeeze.105), kind=kOutput, calls=%fused_computation.20 | convolution fusion | flops 89128960 | bytes 11796480 | tf_op jit(solution)/shard_map/whqk,wkhe->wqhe/dot_general | solution.py:115
  859.1 15.7 %stack.39 = bf16[1,10240,256]{2,1,0:T(8,128)(2,1)} reshape(bf16[640,16,4,64]{3,2,1,0:T(4,128)(2,1)} %copy.169) | data formatting | bytes 10485760 | tf_op jit(solution)/shard_map/stack | solution.py:133
  884.8 15.7 %stack.37 = bf16[1,10240,256]{2,1,0:T(8,128)(2,1)} reshape(bf16[640,16,4,64]{3,2,1,0:T(4,128)(2,1)} %copy.165) | data formatting | bytes 10485760 | tf_op jit(solution)/shard_map/stack | solution.py:133
  910.4 15.8 %stack.38 = bf16[1,10240,256]{2,1,0:T(8,128)(2,1)} reshape(bf16[640,16,4,64]{3,2,1,0:T(4,128)(2,1)} %copy.167) | data formatting | bytes 10485760 | tf_op jit(solution)/shard_map/stack | solution.py:133
  952.1 39.5 %all-reduce = (f32[256]{0:T(256)S(1)}, f32[]{:T(128)}) all-reduce(f32[256]{0:T(256)S(1)} %get-tuple-element.197, f32[]{:T(128)S(6)} %add.251), channel_id=1, replica_groups=mesh['dp'=8,'mp'=4] {'dp','mp'}, use_global_device_ids=true, to_apply=%region_39.40 | all-reduce | flops 257 | bytes 2056 | tf_op jit(solution)/shard_map/psum | solution.py:446
  1003.0 68.4 %all-reduce.14.cloned.1.call-done = (f32[4,256,256]{1,2,0:T(8,128)}, f32[1,256,512]{2,1,0:T(8,128)}) async-done(((f32[4,256,256]{1,2,0:T(8,128)}, f32[1,256,512]{2,1,0:T(8,128)}), (f32[4,256,256]{1,2,0:T(8,128)}, f32[1,256,512]{2,1,0:T(8,128)})) %all-reduce.14.cloned.1.call-update) | async-done | bytes 1572880 | tf_op jit(solution)/shard_map/psum | solution.py:446
  (464 shorter events, 488.3 us)
Async XLA Ops:
  7.2 1081.1 %copy-start = (f32[3,1,64,512]{3,2,1,0:T(8,128)S(1)}, f32[3,1,64,512]{3,2,1,0:T(8,128)}, u32[]{:S(2)}) copy-start(f32[3,1,64,512]{3,2,1,0:T(8,128)} %param.61) | copy-start | bytes 1179652
  7.2 267.1 %all-gather.2.cloned.1.call-start = ((), (), s32[]{:S(2)}) async-start(), calls=%async_computation.3 | async-start | bytes 3276800 | tf_op jit(solution)/shard_map/all_gather | solution.py:337
  8.1 208.9 %copy-start.114 = (f32[640]{0:T(1024)}, f32[640]{0:T(1024)S(1)}, u32[]{:S(2)}) copy-start(f32[640]{0:T(1024)S(1)} %convert_element_type.323) | copy-start | bytes 7684
  8.3 194.9 %copy-start.31 = (pred[640,16]{1,0:T(8,128)(4,1)}, pred[640,16]{1,0:T(8,128)(4,1)S(1)}, u32[]{:S(2)}) copy-start(pred[640,16]{1,0:T(8,128)(4,1)S(1)} %iota_compare_fusion.2) | copy-start | bytes 30724
  20.8 196.1 %copy-start.65 = (bf16[1,256,512]{2,1,0:T(8,128)(2,1)}, bf16[1,256,512]{2,1,0:T(8,128)(2,1)S(1)}, u32[]{:S(2)}) copy-start(bf16[1,256,512]{2,1,0:T(8,128)(2,1)S(1)} %all_gather.40) | copy-start | bytes 786436
  35.1 162.5 %copy-start.17 = (bf16[4,256,256]{2,1,0:T(8,128)(2,1)}, bf16[4,256,256]{2,1,0:T(8,128)(2,1)S(1)}, u32[]{:S(2)}) copy-start(bf16[4,256,256]{2,1,0:T(8,128)(2,1)S(1)} %all_gather.39) | copy-start | bytes 1572868
  221.4 62.3 %all-to-all-start = ((s32[8,3,128]{2,1,0:T(4,128)}), s32[8,3,128]{2,1,0:T(4,128)S(1)}, u32[]{:S(2)}, u32[]{:S(2)}) async-start(s32[8,3,128]{2,1,0:T(4,128)} %all_to_all.12), calls=%async_computation | async-start | bytes 32768 | tf_op jit(solution)/shard_map/all_to_all | solution.py:342
  283.7 65.5 %all-to-all-start.1 = ((bf16[24,128,512]{2,1,0:T(8,128)(2,1)}), bf16[24,128,512]{2,1,0:T(8,128)(2,1)S(1)}, u32[]{:S(2)}, u32[]{:S(2)}) async-start(bf16[24,128,512]{2,1,0:T(8,128)(2,1)} %scatter_fusion), calls=%async_computation.1 | async-start | bytes 6291456 | tf_op jit(solution)/shard_map/all_to_all | solution.py:339
  288.1 144.4 %all-reduce.10.cloned.1.call-start = ((), (), s32[]{:S(2)}) async-start(), calls=%async_computation.4 | async-start | bytes 2097152 | tf_op jit(solution)/shard_map/psum | solution.py:362
  382.6 109.0 %all-reduce.12.cloned.1.call-start = ((), (), s32[]{:S(2)}) async-start(), calls=%async_computation.5 | async-start | bytes 2097152 | tf_op jit(solution)/shard_map/psum | solution.py:392
  440.2 167.7 %all-reduce.18.cloned.1.call-start = ((), (), s32[]{:S(2)}) async-start(), calls=%async_computation.8 | async-start | bytes 4194304 | tf_op jit(solution)/shard_map/psum | solution.py:373
  521.3 86.6 %copy-start.93 = (f32[1024]{0:T(1024)S(1)}, f32[1024]{0:T(1024)}, u32[]{:S(2)}) copy-start(f32[1024]{0:T(1024)} %copy-done.92) | copy-start | bytes 12292
  521.3 86.6 %copy-start.99 = (f32[1,512]{1,0:T(1,128)S(1)}, f32[1,512]{1,0:T(1,128)}, u32[]{:S(2)}) copy-start(f32[1,512]{1,0:T(1,128)} %get-tuple-element.237) | copy-start | bytes 6148
  630.5 107.4 %all-to-all-start.2 = ((bf16[24,128,512]{2,1,0:T(8,128)(2,1)}), bf16[24,128,512]{2,1,0:T(8,128)(2,1)}, u32[]{:S(2)}, u32[]{:S(2)}) async-start(bf16[24,128,512]{2,1,0:T(8,128)(2,1)} %broadcast_select_fusion), calls=%async_computation.2 | async-start | bytes 6291456 | tf_op jit(solution)/shard_map/all_to_all | solution.py:424
  635.0 79.1 %all-reduce.16.cloned.1.call-start = ((), (), s32[]{:S(2)}) async-start(), calls=%async_computation.7 | async-start | bytes 3145728 | tf_op jit(solution)/shard_map/psum | solution.py:434
  639.9 96.7 %copy-start.38 = (bf16[1024,512]{1,0:T(8,128)(2,1)S(1)}, bf16[1024,512]{1,0:T(8,128)(2,1)}, u32[]{:S(2)}) copy-start(bf16[1024,512]{1,0:T(8,128)(2,1)} %get-tuple-element.211) | copy-start | bytes 3145732
  641.4 82.6 %copy-start.111 = (bf16[512]{0:T(512)(128)(2,1)S(1)}, bf16[512]{0:T(512)(128)(2,1)}, u32[]{:S(2)}) copy-start(bf16[512]{0:T(512)(128)(2,1)} %get-tuple-element.199) | copy-start | bytes 3076
  641.4 430.0 %all-reduce.14.cloned.1.call-start = ((), (), s32[]{:S(2)}) async-start(), calls=%async_computation.6 | async-start | bytes 3145728 | tf_op jit(solution)/shard_map/psum | solution.py:446
  1002.3 78.6 %copy-start.103 = (bf16[2,512]{1,0:T(2,128)(2,1)S(1)}, bf16[2,512]{1,0:T(2,128)(2,1)}, u32[]{:S(2)}) copy-start(bf16[2,512]{1,0:T(2,128)(2,1)} %copy-done.102) | copy-start | bytes 6148
  1002.3 78.6 %copy-start.104 = (f32[2,512]{1,0:T(2,128)S(1)}, f32[2,512]{1,0:T(2,128)}, u32[]{:S(2)}) copy-start(f32[2,512]{1,0:T(2,128)} %param.47) | copy-start | bytes 12292
  1002.4 79.2 %copy-start.16 = (bf16[1,128,512]{2,1,0:T(8,128)(2,1)S(1)}, bf16[1,128,512]{2,1,0:T(8,128)(2,1)}, u32[]{:S(2)}) copy-start(bf16[1,128,512]{2,1,0:T(8,128)(2,1)} %get-tuple-element.208) | copy-start | bytes 393220
  1002.4 79.3 %copy-start.12 = (bf16[3,1,512,128]{2,3,0,1:T(8,128)(2,1)S(1)}, bf16[3,1,512,128]{2,3,0,1:T(8,128)(2,1)}, u32[]{:S(2)}) copy-start(bf16[3,1,512,128]{2,3,0,1:T(8,128)(2,1)} %get-tuple-element.207) | copy-start | bytes 1179652
  1002.4 80.3 %copy-start.10 = (bf16[1,512,512]{2,1,0:T(8,128)(2,1)S(1)}, bf16[1,512,512]{2,1,0:T(8,128)(2,1)}, u32[]{:S(2)}) copy-start(bf16[1,512,512]{2,1,0:T(8,128)(2,1)} %get-tuple-element.209) | copy-start | bytes 1572868
  1002.4 80.3 %copy-start.11 = (bf16[1,512,512]{2,1,0:T(8,128)(2,1)S(1)}, bf16[1,512,512]{2,1,0:T(8,128)(2,1)}, u32[]{:S(2)}) copy-start(bf16[1,512,512]{2,1,0:T(8,128)(2,1)} %get-tuple-element.210) | copy-start | bytes 1572868
  (114 other events, 1386.7 us)
Sparse Core Ops, SparseCore 0:
  219.2 55.0 all-gather.1
  382.8 49.7 all-reduce.9
  440.4 51.1 all-reduce.11
  521.5 86.4 all-reduce.17
  641.5 72.5 all-reduce.15
  939.9 131.4 all-reduce.13
where the time goes:
time: 1150 us; the launch traced here: 1140 us
  waiting for transfers between devices  248 us (22%)
  blocking collectives  240 us (21%)
  local copies, waits for them, and re-layouts  238 us (21%)
  matrix products  220 us (19%)
  other arithmetic  160 us (14%)
  between operations  22.9 us (2%)
  starting transfers between devices  12.5 us (1%)
    psum x1, waiting for transfers between devices, local(): lax.psum((grad_mixer, grad_lift, grad_char_gain, word_squares), ('dp', 'm...  68.4 us
    all_gather x1, waiting for transfers between devices, local(): whole_vectors = lax.all_gather(vector_blocks, 'mp', axis=1, tiled=True)  49.6 us
    another operation x4, local copies, waits for them, and re-layouts, char_backward(): jnp.stack([grad_queries, grad_keys, grad_values]).astype(jnp.bfloat16)  48.4 us
    psum x1, waiting for transfers between devices, local(): lax.psum(part_two.astype(jnp.bfloat16), 'mp').astype(jnp.float32)  47.8 us
    all_gather x1, blocking collectives, local(): lax.all_gather(char_lift_right_root.astype(jnp.bfloat16), 'dp', axis=1, t...  43.4 us
    all_gather x1, blocking collectives, local(): lax.all_gather(word_project.astype(jnp.bfloat16), 'dp', axis=2, tiled=True)  40.4 us
    psum x1, blocking collectives, local(): lax.psum((grad_mixer, grad_lift, grad_char_gain, word_squares), ('dp', 'm...  39.5 us
    psum x1, waiting for transfers between devices, local(): lax.psum(jnp.dot(active, lower_mats[0], preferred_element_type=jnp.float3...  36.8 us
  transfers between devices with their start and end apart: 9, of which 6 were waited for; matrix products, arithmetic and copies ran while one was open for 6% of the time, Pallas kernels for 0%

commit v1 on v0

v1 whole, which is shorter than its diff:
```python
import functools
import math

import jax
import jax.numpy as jnp
from jax import lax
from jax.experimental import pallas as pl
from jax.experimental.pallas import tpu as pltpu
from jax.sharding import PartitionSpec as P

D = 512
HD = 64
FF = 2048
CHAR_BLOCK_WIDTH = 256
OWNER_BLOCKS = 10
decay_rate = 0.5
learn_rate = 1.0
gain_rate = 0.4
negative_big = -1e30

CW = 256
CHEADS = 4
CHD = 64
SPOTS = 16
KEPT = 3 * CW + CHEADS * 128 + CW
epsilon = 1e-05
BF = jnp.bfloat16
F32 = jnp.float32


def nn(a, b):
    return lax.dot_general(a, b, (((1,), (0,)), ((), ())), preferred_element_type=F32)


def nt(a, b):
    return lax.dot_general(a, b, (((1,), (1,)), ((), ())), preferred_element_type=F32)


def tn(a, b):
    return lax.dot_general(a, b, (((0,), (0,)), ((), ())), preferred_element_type=F32)


def char_classes(share):
    listed = [(1, 4, 32), (2, 8, 16), (4, 16, 8)]
    return [c for c in listed if c[2] <= share]


def order_matrix(places, words):
    row = lax.broadcasted_iota(jnp.int32, (128, SPOTS * words), 0)
    col = lax.broadcasted_iota(jnp.int32, (128, SPOTS * words), 1)
    return ((row % words) * SPOTS + row // words == col).astype(BF)


def head_stack(rows, scale):
    lane = lax.broadcasted_iota(jnp.int32, (1, CW), 1) // CHD
    return jnp.concatenate(
        [rows * jnp.where(lane == h, scale, 0.0).astype(BF) for h in range(CHEADS)], axis=0
    )


def char_forward_kernel(
    classes, kind, x_ref, count_ref, gain_ref, mats_ref, *refs
):
    orders = refs[: len(classes)]
    vec_ref, kept_ref, pooled_ref, msum_ref, sumx, counts = refs[len(classes) :]
    step = pl.program_id(0)
    share = count_ref.shape[1]
    own = pl.ds(pl.multiple_of(step * share, share), share)
    counts[own, :] = count_ref[0]

    @pl.when(kind[step] == 0)
    def _():
        sumx[own, :] = jnp.zeros((share, CW), F32)
        msum_ref[own, :] = jnp.zeros((share, CW), F32)

    def block(places, words, order_ref):
        groups = share // words
        kept_x = []
        normed = []
        for g in range(groups):
            x = nn(order_ref[...], x_ref[0, pl.ds(g * words * SPOTS, words * SPOTS), :])
            scale = lax.rsqrt(jnp.mean(x * x, axis=-1, keepdims=True) + epsilon)
            normed.append((x * scale * gain_ref[...]).astype(BF))
            cnt = count_ref[0, pl.ds(g * words, words), :]
            cnt2 = jnp.concatenate([cnt, cnt], axis=1)
            place = lax.broadcasted_iota(jnp.int32, (places, words, CW), 0).astype(F32)
            x3 = x.reshape(places, words, CW)
            sumx[pl.ds(pl.multiple_of(step * share + g * words, words), words), :] = jnp.sum(
                jnp.where(place < cnt2[None], x3, 0.0), axis=0
            )
        rows = groups * 128
        normed = jnp.concatenate(normed, axis=0) if groups > 1 else normed[0]
        for t in range(3):
            kept_ref[0, :rows, t * CW : (t + 1) * CW] = nn(
                normed, mats_ref[:, t * CW : (t + 1) * CW]
            ).astype(BF)
        lane = lax.broadcasted_iota(jnp.int32, (words, CHEADS * 128), 1) % 128
        word = lax.broadcasted_iota(jnp.int32, (words, CHEADS * 128), 0)
        mine = lane % words == word
        spot = (lane // words).astype(F32)
        head_row = lax.broadcasted_iota(jnp.int32, (CHEADS * 128, CW), 0) // 128
        head_col = lax.broadcasted_iota(jnp.int32, (CHEADS * 128, CW), 1) // CHD
        same_head = (head_row == head_col).astype(BF)
        for g in range(groups):
            at = g * 128
            q = kept_ref[0, at : at + 128, :CW]
            k = kept_ref[0, at : at + 128, CW : 2 * CW]
            v = kept_ref[0, at : at + 128, 2 * CW : 3 * CW]
            s = nt(k, head_stack(q, 1.0 / math.sqrt(CHD))).reshape(places, words, CHEADS * 128)
            cnt = count_ref[0, pl.ds(g * words, words), :]
            cnt4 = jnp.concatenate([cnt] * CHEADS, axis=1)
            place = lax.broadcasted_iota(jnp.int32, (places, words, CHEADS * 128), 0).astype(F32)
            s = jnp.where(place < cnt4[None], s, -1e30)
            e = jnp.exp(s - jnp.max(s, axis=0)[None])
            r = jnp.where(mine & (spot < cnt4), 1.0 / jnp.sum(e, axis=0), 0.0)
            p = (e * r[None]).astype(BF).reshape(128, CHEADS * 128)
            kept_ref[0, at : at + 128, 3 * CW : 3 * CW + CHEADS * 128] = p
            c = nn(p, same_head)
            kept_ref[0, at : at + 128, 3 * CW + CHEADS * 128 :] = c.astype(BF)
            msum_ref[pl.ds(pl.multiple_of(step * share + g * words, words), words), :] = jnp.sum(
                (c * v.astype(F32)).reshape(places, words, CW), axis=0
            )

    for (number, places, words), order_ref in zip(classes, orders):
        pl.when(kind[step] == number)(functools.partial(block, places, words, order_ref))

    @pl.when(step == pl.num_programs(0) - 1)
    def _():
        cnt2 = jnp.concatenate([counts[...]] * 2, axis=1)
        summed = sumx[...] + nn(msum_ref[...].astype(BF), mats_ref[:, 3 * CW : 4 * CW])
        pooled = (summed / cnt2).astype(BF)
        pooled_ref[...] = pooled
        vec_ref[...] = nn(pooled, mats_ref[:, 4 * CW :]).astype(BF)


def char_kind(block_home, char_count, share):
    places = jnp.max(char_count, axis=1)
    kind = jnp.where(places <= 8, 2, 4)
    if share >= 32:
        kind = jnp.where(places <= 4, 1, kind)
    return jnp.where(block_home >= 0, kind, 0).astype(jnp.int32)


def whole(shape):
    return pl.BlockSpec(shape, lambda i, *_: (0,) * len(shape))


def char_forward(x, kind, counts, gain, mats):
    slots, share = x.shape[:2]
    classes = char_classes(share)
    rows = share * SPOTS
    orders = [order_matrix(p, w) for _, p, w in classes]
    words_all = slots * share
    per_slot = lambda shape: pl.BlockSpec((1,) + shape, lambda i, *_: (i,) + (0,) * len(shape))
    return pl.pallas_call(
        functools.partial(char_forward_kernel, classes),
        grid_spec=pltpu.PrefetchScalarGridSpec(
            num_scalar_prefetch=1,
            grid=(slots,),
            in_specs=[
                per_slot((rows, CW)),
                per_slot((share, 128)),
                whole((1, CW)),
                whole(mats.shape),
            ]
            + [whole(o.shape) for o in orders],
            out_specs=[
                whole((words_all, D)),
                per_slot((rows, KEPT)),
                whole((words_all, CW)),
                whole((words_all, CW)),
            ],
            scratch_shapes=[
                pltpu.VMEM((words_all, CW), F32),
                pltpu.VMEM((words_all, 128), F32),
            ],
        ),
        out_shape=[
            jax.ShapeDtypeStruct((words_all, D), BF),
            jax.ShapeDtypeStruct((slots, rows, KEPT), BF),
            jax.ShapeDtypeStruct((words_all, CW), BF),
            jax.ShapeDtypeStruct((words_all, CW), F32),
        ],
        compiler_params=pltpu.CompilerParams(vmem_limit_bytes=40 << 20),
        cost_estimate=pl.CostEstimate(
            flops=slots * rows * CW * CW * 16, bytes_accessed=slots * rows * KEPT * 3, transcendentals=0
        ),
        name="char_forward",
    )(kind, x.reshape(slots, rows, CW), counts, gain.reshape(1, CW), mats, *orders)


def char_backward_kernel(
    classes, kind, x_ref, count_ref, kept_ref, all_counts_ref, gv_ref, pooled_ref, msum_ref,
    gain_ref, mats_ref, *refs
):
    orders = refs[: len(classes)]
    dx_ref, dqkv_ref, dout_ref, dlift_ref, dgain_ref, gp_all, gm_all, dh, normed_all = refs[len(classes) :]
    step = pl.program_id(0)
    share = count_ref.shape[1]
    base = step * share

    @pl.when(step == 0)
    def _():
        gv = gv_ref[...]
        cnt2 = jnp.concatenate([all_counts_ref[...]] * 2, axis=1)
        gp = nt(gv, mats_ref[:, 4 * CW :]) / cnt2
        gp_all[...] = gp
        gpb = gp.astype(BF)
        gm_all[...] = nt(gpb, mats_ref[:, 3 * CW : 4 * CW]).astype(BF).astype(F32)
        dlift_ref[...] = tn(pooled_ref[...], gv)
        dout_ref[...] = tn(msum_ref[...].astype(BF), gpb)
        dqkv_ref[...] = jnp.zeros_like(dqkv_ref)
        dgain_ref[...] = jnp.zeros_like(dgain_ref)

    @pl.when(kind[step] == 0)
    def _():
        dx_ref[...] = jnp.zeros_like(dx_ref)

    def block(places, words, order_ref):
        groups = share // words
        rows = groups * 128
        gain = gain_ref[...]
        xs = []
        scales = []
        gps = []
        for g in range(groups):
            at = g * 128
            x = nn(order_ref[...], x_ref[0, pl.ds(g * words * SPOTS, words * SPOTS), :])
            scale = lax.rsqrt(jnp.mean(x * x, axis=-1, keepdims=True) + epsilon)
            normed_all[at : at + 128, :] = (x * scale * gain).astype(BF)
            xs.append(x)
            scales.append(scale)
            mine = pl.ds(pl.multiple_of(base + g * words, words), words)
            cnt = count_ref[0, pl.ds(g * words, words), :]
            cnt2 = jnp.concatenate([cnt, cnt], axis=1)
            place = lax.broadcasted_iota(jnp.int32, (places, words, CW), 0).astype(F32)
            shown = place < cnt2[None]
            gps.append(jnp.where(shown, gp_all[mine, :][None], 0.0).reshape(128, CW))
            gm_word = gm_all[mine, :]
            gm = jnp.where(shown, gm_word[None], 0.0).reshape(128, CW).astype(BF)
            q = kept_ref[0, at : at + 128, :CW]
            k = kept_ref[0, at : at + 128, CW : 2 * CW]
            v = kept_ref[0, at : at + 128, 2 * CW : 3 * CW]
            p = kept_ref[0, at : at + 128, 3 * CW : 3 * CW + CHEADS * 128].astype(F32)
            c = kept_ref[0, at : at + 128, 3 * CW + CHEADS * 128 :].astype(F32)
            dp = nt(v, head_stack(gm, 1.0))
            p3 = p.reshape(places, words, CHEADS * 128)
            t = p3 * dp.reshape(places, words, CHEADS * 128)
            ds = (t - p3 * jnp.sum(t, axis=0)[None]).astype(BF).reshape(128, CHEADS * 128)
            eighth = 1.0 / math.sqrt(CHD)
            dk = nn(ds, head_stack(q, eighth))
            ds_rows = jnp.concatenate([ds[:, h * 128 : (h + 1) * 128] for h in range(CHEADS)], axis=0)
            dq = tn(ds_rows, head_stack(k, eighth))
            dv = (c.reshape(places, words, CW) * gm_word[None]).reshape(128, CW)
            dh[at : at + 128, :CW] = dq.astype(BF)
            dh[at : at + 128, CW : 2 * CW] = dk.astype(BF)
            dh[at : at + 128, 2 * CW :] = dv.astype(BF)
        grads = dh[:rows, :]
        dqkv_ref[...] += tn(normed_all[:rows, :], grads)
        dn_all = nt(grads, mats_ref[:, : 3 * CW])
        dgain = jnp.zeros((1, CW), F32)
        for g in range(groups):
            x, scale = xs[g], scales[g]
            dn = dn_all[g * 128 : (g + 1) * 128]
            xr = x * scale
            dgain = dgain + jnp.sum(xr * dn, axis=0, keepdims=True)
            w = dn * gain
            inner = jnp.mean(xr * w, axis=-1, keepdims=True)
            dx = gps[g] + scale * (w - xr * inner)
            dx_ref[0, pl.ds(g * words * SPOTS, words * SPOTS), :] = tn(
                order_ref[...], dx.astype(BF)
            ).astype(BF)
        dgain_ref[...] += dgain

    for (number, places, words), order_ref in zip(classes, orders):
        pl.when(kind[step] == number)(functools.partial(block, places, words, order_ref))


def char_backward(x, kind, counts, gain, mats, kept, pooled, msum, grad_vectors):
    slots, share = x.shape[:2]
    classes = char_classes(share)
    rows = share * SPOTS
    orders = [order_matrix(p, w) for _, p, w in classes]
    words_all = slots * share
    per_slot = lambda shape: pl.BlockSpec((1,) + shape, lambda i, *_: (i,) + (0,) * len(shape))
    dx, dqkv, dout, dlift, dgain = pl.pallas_call(
        functools.partial(char_backward_kernel, classes),
        grid_spec=pltpu.PrefetchScalarGridSpec(
            num_scalar_prefetch=1,
            grid=(slots,),
            in_specs=[
                per_slot((rows, CW)),
                per_slot((share, 128)),
                per_slot((rows, KEPT)),
                whole((words_all, 128)),
                whole((words_all, D)),
                whole((words_all, CW)),
                whole((words_all, CW)),
                whole((1, CW)),
                whole(mats.shape),
            ]
            + [whole(o.shape) for o in orders],
            out_specs=[
                per_slot((rows, CW)),
                whole((CW, 3 * CW)),
                whole((CW, CW)),
                whole((CW, D)),
                whole((1, CW)),
            ],
            scratch_shapes=[
                pltpu.VMEM((words_all, CW), F32),
                pltpu.VMEM((words_all, CW), F32),
                pltpu.VMEM((rows, 3 * CW), BF),
                pltpu.VMEM((rows, CW), BF),
            ],
        ),
        out_shape=[
            jax.ShapeDtypeStruct((slots, rows, CW), BF),
            jax.ShapeDtypeStruct((CW, 3 * CW), F32),
            jax.ShapeDtypeStruct((CW, CW), F32),
            jax.ShapeDtypeStruct((CW, D), F32),
            jax.ShapeDtypeStruct((1, CW), F32),
        ],
        compiler_params=pltpu.CompilerParams(vmem_limit_bytes=40 << 20),
        cost_estimate=pl.CostEstimate(
            flops=slots * rows * CW * CW * 28, bytes_accessed=slots * rows * KEPT * 3, transcendentals=0
        ),
        name="char_backward",
    )(
        kind, x.reshape(slots, rows, CW), counts, kept, counts.reshape(words_all, 128), grad_vectors,
        pooled, msum, gain.reshape(1, CW), mats, *orders,
    )
    return dx.reshape(x.shape), dqkv, dout, dlift, dgain


def norm_forward(values, gain_row):
    row_scale = lax.rsqrt(jnp.mean(values * values, axis=-1, keepdims=True) + epsilon)
    return (values * row_scale * gain_row, row_scale)


def norm_backward(values, row_scale, gain_row, grad_output):
    weighted = grad_output * gain_row
    row_inner = jnp.mean(values * weighted, axis=-1, keepdims=True)
    grad_values = row_scale * weighted - values * (row_scale * row_scale * row_scale) * row_inner
    return (grad_values, jnp.sum(values * row_scale * grad_output, axis=0))


def gelu_tanh(values):
    return jax.nn.gelu(values, approximate=True)


def word_softmax(row_queries, row_keys, query_docs, key_docs, first_row):
    scores = jnp.einsum(
        "qhe,khe->hqk", row_queries, row_keys, preferred_element_type=jnp.float32
    ) / math.sqrt(HD)
    table_shape = (row_queries.shape[0], row_keys.shape[0])
    query_at = first_row + lax.broadcasted_iota(jnp.int32, table_shape, 0)
    key_at = lax.broadcasted_iota(jnp.int32, table_shape, 1)
    allowed = (key_at <= query_at) & (key_docs[None, :] == query_docs[:, None])
    return jax.nn.softmax(jnp.where(allowed[None], scores, negative_big), axis=-1)


def word_attention(queries, keys_all, values_all, documents):
    length = queries.shape[1]
    block_rows = min(512, length)

    def one_row(pieces):
        row_queries, row_keys, row_values, row_docs = pieces
        outputs = []
        for first_row in range(0, length, block_rows):
            last_row = first_row + block_rows
            attention = word_softmax(
                row_queries[first_row:last_row],
                row_keys,
                row_docs[first_row:last_row],
                row_docs,
                first_row,
            )
            outputs.append(
                jnp.einsum(
                    "hqk,khe->qhe",
                    attention.astype(jnp.bfloat16),
                    row_values,
                    preferred_element_type=jnp.float32,
                ).astype(jnp.bfloat16)
            )
        return jnp.concatenate(outputs, axis=0)

    return lax.map(one_row, (queries, keys_all, values_all, documents))


def word_attention_back(queries, keys_all, values_all, grad_mixed, documents):
    length = queries.shape[1]
    block_rows = min(512, length)
    root_size = math.sqrt(HD)

    def one_row(pieces):
        row_queries, row_keys, row_values, row_grads, row_docs = pieces
        query_parts = []
        grad_keys = jnp.zeros(row_keys.shape, jnp.float32)
        grad_values = jnp.zeros(row_values.shape, jnp.float32)
        for first_row in range(0, length, block_rows):
            last_row = first_row + block_rows
            attention = word_softmax(
                row_queries[first_row:last_row],
                row_keys,
                row_docs[first_row:last_row],
                row_docs,
                first_row,
            )
            grad_attention = jnp.einsum(
                "qhe,khe->hqk",
                row_grads[first_row:last_row],
                row_values,
                preferred_element_type=jnp.float32,
            )
            row_inner = jnp.sum(attention * grad_attention, axis=-1, keepdims=True)
            grad_scores = (attention * (grad_attention - row_inner)).astype(jnp.bfloat16)
            query_parts.append(
                jnp.einsum(
                    "hqk,khe->qhe", grad_scores, row_keys, preferred_element_type=jnp.float32
                )
                / root_size
            )
            grad_keys = (
                grad_keys
                + jnp.einsum(
                    "hqk,qhe->khe",
                    grad_scores,
                    row_queries[first_row:last_row],
                    preferred_element_type=jnp.float32,
                )
                / root_size
            )
            grad_values = grad_values + jnp.einsum(
                "hqk,qhe->khe",
                attention.astype(jnp.bfloat16),
                row_grads[first_row:last_row],
                preferred_element_type=jnp.float32,
            )
        grad_queries = jnp.concatenate(query_parts, axis=0)
        return (
            grad_queries.astype(jnp.bfloat16),
            grad_keys.astype(jnp.bfloat16),
            grad_values.astype(jnp.bfloat16),
        )

    return lax.map(one_row, (queries, keys_all, values_all, grad_mixed, documents))


def pack(array):
    rows, cols = array.shape[-2:]
    if cols % 128:
        return array.reshape(-1, 128)
    split = array.reshape(-1, rows, cols // 128, 128)
    return split.transpose(0, 2, 1, 3).reshape(-1, 128)


def unpack(gathered, shapes):
    devices = gathered.shape[0]
    whole_ones = []
    first = 0
    for shape in shapes:
        lead, (rows, cols) = shape[:-2], shape[-2:]
        count = math.prod(shape) // 128
        piece = gathered[:, first : first + count]
        first += count
        if cols % 128:
            piece = piece.reshape(devices, -1, rows, cols).transpose(1, 0, 2, 3)
        else:
            piece = piece.reshape(devices, -1, cols // 128, rows, 128).transpose(1, 0, 3, 2, 4)
        whole_ones.append(piece.reshape(lead + (devices * rows, cols)))
    return whole_ones


def refresh(master, gradient, left_stat, right_stat, left_root, right_root, factor, owner_index):
    clipped = gradient * factor
    near = clipped.astype(BF)
    rows_own = master.shape[-2]
    cols_own = right_stat.shape[-2]
    own_rows = lax.dynamic_slice_in_dim(clipped, owner_index * rows_own, rows_own, clipped.ndim - 2)
    own_cols = lax.dynamic_slice_in_dim(near, owner_index * cols_own, cols_own, clipped.ndim - 1)
    left_new = decay_rate * left_stat + (1.0 - decay_rate) * jnp.einsum(
        "...mn,...kn->...mk", own_rows.astype(BF), near, preferred_element_type=F32
    )
    right_new = decay_rate * right_stat + (1.0 - decay_rate) * jnp.einsum(
        "...mn,...mk->...nk", own_cols, near, preferred_element_type=F32
    )
    half_step = jnp.matmul(left_root.astype(BF), near, preferred_element_type=F32)
    shampoo_step = jnp.matmul(half_step.astype(BF), right_root, preferred_element_type=F32)
    fresh_master = master - learn_rate * shampoo_step
    return (own_rows, left_new, right_new, fresh_master, fresh_master.astype(BF))


def local(
    word_inputs,
    character_embeddings,
    cotangent,
    char_count,
    word_place,
    block_home,
    documents,
    char_gain,
    word_gains,
    char_mixer,
    char_mixer_left,
    char_mixer_right,
    char_mixer_left_root,
    char_mixer_right_root,
    char_lift,
    char_lift_left,
    char_lift_right,
    char_lift_left_root,
    char_lift_right_root,
    word_project,
    word_project_left,
    word_project_right,
    word_project_left_root,
    word_project_right_root,
    word_output,
    word_output_left,
    word_output_right,
    word_output_left_root,
    word_output_right_root,
    feed_upper,
    feed_upper_left,
    feed_upper_right,
    feed_upper_left_root,
    feed_upper_right_root,
    feed_lower,
    feed_lower_left,
    feed_lower_right,
    feed_lower_left_root,
    feed_lower_right_root,
):
    slot_count, share_rows = (character_embeddings.shape[0], character_embeddings.shape[1])
    peer_count = lax.axis_size("dp")
    part_count = lax.axis_size("mp")
    owner_index = lax.axis_index("dp")
    pair_cap = -(-slot_count // peer_count)
    slot_total = peer_count * pair_cap
    rows_dev, length = (word_inputs.shape[0], word_inputs.shape[1])
    words_dev = rows_dev * length
    block_words = share_rows * part_count

    char_pack = jnp.concatenate(
        [char_mixer[0], char_mixer[1], char_mixer[2], char_mixer[3], char_lift[0]], axis=1
    ).astype(BF)
    char_whole = lax.all_gather(char_pack, "dp", axis=0, tiled=True)
    word_whole = lax.all_gather(
        jnp.concatenate([pack(w) for w in (word_project, word_output, feed_upper, feed_lower)]).astype(BF),
        "dp",
        axis=0,
    )
    project_mats, output_mats, upper_mats, lower_mats = unpack(
        word_whole, [w.shape for w in (word_project, word_output, feed_upper, feed_lower)]
    )
    roots = (
        char_mixer_right_root,
        char_lift_right_root,
        word_project_right_root,
        word_output_right_root,
        feed_upper_right_root,
        feed_lower_right_root,
    )
    root_whole = lax.all_gather(
        jnp.concatenate([pack(w) for w in roots]).astype(BF), "dp", axis=0
    )

    peers = lax.broadcasted_iota(jnp.int32, (slot_count, peer_count), 1)
    owner_match = (block_home[:, None] == peers).astype(jnp.int32)
    earlier = (
        lax.broadcasted_iota(jnp.int32, (slot_count, slot_count), 1)
        < lax.broadcasted_iota(jnp.int32, (slot_count, slot_count), 0)
    )
    same_owner = block_home[:, None] == block_home[None, :]
    slot_rank = jnp.sum((earlier & same_owner).astype(jnp.int32), axis=1)
    slot_target = jnp.where(block_home >= 0, block_home * pair_cap + slot_rank, slot_total)
    to_slot = lax.broadcasted_iota(jnp.int32, (slot_total, slot_count), 0) == slot_target[None, :]

    kind = char_kind(block_home, char_count, share_rows)
    counts = jnp.broadcast_to(
        char_count.astype(F32)[..., None], (slot_count, share_rows, 128)
    )
    word_vectors, kept, pooled, msum = char_forward(
        character_embeddings, kind, counts, char_gain, char_whole
    )

    sent_place = jnp.max(
        jnp.where(to_slot[:, :, None], word_place[None] + 1, 0), axis=1
    ) - 1
    came_place = lax.all_to_all(sent_place, "dp", split_axis=0, concat_axis=0, tiled=True)
    live = jnp.max(came_place, axis=1) >= 0
    slots_before = (
        lax.broadcasted_iota(jnp.int32, (slot_total, slot_total), 1)
        < lax.broadcasted_iota(jnp.int32, (slot_total, slot_total), 0)
    )
    live_rank = jnp.sum((slots_before & live[None, :]).astype(jnp.int32), axis=1)
    live_rank = jnp.where(live, live_rank, OWNER_BLOCKS)
    to_live = lax.broadcasted_iota(jnp.int32, (OWNER_BLOCKS, slot_total), 0) == live_rank[None, :]
    live_place = jnp.max(jnp.where(to_live[:, :, None], came_place[None] + 1, 0), axis=1) - 1

    wide = share_rows * D
    sent = jnp.dot(
        to_slot.astype(BF), word_vectors.reshape(slot_count, wide), preferred_element_type=F32
    ).astype(BF)
    came = lax.all_to_all(
        sent.reshape(slot_total, share_rows, D), "dp", split_axis=0, concat_axis=0, tiled=True
    )
    compact = jnp.dot(
        to_live.astype(BF), came.reshape(slot_total, wide), preferred_element_type=F32
    ).astype(BF)
    live_vectors = lax.all_gather(compact.reshape(OWNER_BLOCKS * share_rows, D), "mp", axis=0)
    place_parts = live_place.reshape(OWNER_BLOCKS, part_count, share_rows)
    place_flat = place_parts.transpose(1, 0, 2).reshape(-1)
    numbers = lax.broadcasted_iota(jnp.int32, (words_dev, place_flat.shape[0]), 0)
    placed = jnp.dot(
        (numbers == place_flat[None, :]).astype(BF),
        live_vectors.reshape(-1, D),
        preferred_element_type=F32,
    )
    stream = word_inputs.reshape(words_dev, D).astype(F32) + placed
    normed_float, scale_one = norm_forward(stream, word_gains[0])
    normed_one = normed_float.astype(BF)
    block_width = output_mats.shape[1]
    local_heads = block_width // HD
    projected = jnp.einsum(
        "rd,tde->tre", normed_one, project_mats[:, 0], preferred_element_type=F32
    ).astype(BF)
    heads_view = projected.reshape(3, rows_dev, length, local_heads, HD)
    mixed_rows = word_attention(heads_view[0], heads_view[1], heads_view[2], documents).reshape(
        words_dev, block_width
    )
    attend_total = lax.psum(
        jnp.dot(mixed_rows, output_mats[0], preferred_element_type=F32).astype(BF), "mp"
    ).astype(F32)
    hidden = stream + attend_total
    normed_float_two, scale_two = norm_forward(hidden, word_gains[1])
    normed_two = normed_float_two.astype(BF)
    upper_rows = jnp.dot(normed_two, upper_mats[0], preferred_element_type=F32)
    active = gelu_tanh(upper_rows).astype(BF)
    feed_total = lax.psum(
        jnp.dot(active, lower_mats[0], preferred_element_type=F32).astype(BF), "mp"
    ).astype(F32)
    block_out = (hidden + feed_total).astype(BF).reshape(word_inputs.shape)
    grad_output = cotangent.reshape(words_dev, D).astype(F32)
    grad_feed = grad_output.astype(BF)
    grad_lower = jnp.einsum("rf,rd->fd", active, grad_feed, preferred_element_type=F32)
    grad_active = jnp.einsum("rd,fd->rf", grad_feed, lower_mats[0], preferred_element_type=F32)
    unused_value, gelu_pull = jax.vjp(gelu_tanh, upper_rows)
    grad_upper_rows = gelu_pull(grad_active)[0].astype(BF)
    grad_upper = jnp.einsum("rd,rf->df", normed_two, grad_upper_rows, preferred_element_type=F32)
    part_two = jnp.einsum("rf,df->rd", grad_upper_rows, upper_mats[0], preferred_element_type=F32)
    grad_normed_two = lax.psum(part_two.astype(BF), "mp").astype(F32)
    grad_hidden_norm, gain_two = norm_backward(hidden, scale_two, word_gains[1], grad_normed_two)
    grad_hidden = grad_output + grad_hidden_norm
    grad_attend = grad_hidden.astype(BF)
    grad_output_mat = jnp.einsum("re,rd->ed", mixed_rows, grad_attend, preferred_element_type=F32)
    grad_mixed = jnp.einsum(
        "rd,ed->re", grad_attend, output_mats[0], preferred_element_type=F32
    ).astype(BF)
    grad_queries, grad_keys, grad_values = word_attention_back(
        heads_view[0],
        heads_view[1],
        heads_view[2],
        grad_mixed.reshape(rows_dev, length, local_heads, HD),
        documents,
    )
    grad_heads = jnp.stack([grad_queries, grad_keys, grad_values]).reshape(3, words_dev, block_width)
    grad_project = jnp.einsum("rd,tre->tde", normed_one, grad_heads, preferred_element_type=F32)
    part_one = jnp.einsum(
        "tre,tde->rd", grad_heads, project_mats[:, 0], preferred_element_type=F32
    )
    grad_normed_one = lax.psum(part_one.astype(BF), "mp").astype(F32)
    grad_stream_norm, gain_one = norm_backward(stream, scale_one, word_gains[0], grad_normed_one)
    grad_stream = grad_hidden + grad_stream_norm
    grad_words = grad_stream.astype(BF)
    word_inputs_gradient = grad_words.reshape(word_inputs.shape)

    own_place = lax.dynamic_slice_in_dim(
        came_place.reshape(slot_total, part_count, share_rows), lax.axis_index("mp"), 1, 1
    ).reshape(-1)
    picked = jnp.dot(
        (
            own_place[:, None]
            == lax.broadcasted_iota(jnp.int32, (own_place.shape[0], words_dev), 1)
        ).astype(BF),
        grad_words,
        preferred_element_type=F32,
    ).astype(BF)
    returned = lax.all_to_all(
        picked.reshape(slot_total, share_rows, D), "dp", split_axis=0, concat_axis=0, tiled=True
    )
    grad_vectors = (
        jnp.dot(to_slot.astype(BF).T, returned.reshape(slot_total, wide), preferred_element_type=F32)
        .astype(BF)
        .reshape(slot_count * share_rows, D)
    )
    char_embeds_gradient, grad_wide, grad_out, grad_lift, grad_char_gain = char_backward(
        character_embeddings, kind, counts, char_gain, char_whole, kept, pooled, msum, grad_vectors
    )
    sum_project, sum_output, sum_upper, sum_lower, sum_word_gains = (
        s.astype(F32)
        for s in lax.psum(
            (
                grad_project[:, None].astype(BF),
                grad_output_mat[None].astype(BF),
                grad_upper[None].astype(BF),
                grad_lower[None].astype(BF),
                jnp.stack([gain_one, gain_two]).astype(BF),
            ),
            "dp",
        )
    )
    word_squares = (
        jnp.sum(sum_project * sum_project)
        + jnp.sum(sum_output * sum_output)
        + jnp.sum(sum_upper * sum_upper)
        + jnp.sum(sum_lower * sum_lower)
    )
    sum_wide, sum_out, sum_lift, sum_char_gain, spread_squares = lax.psum(
        (grad_wide, grad_out, grad_lift, grad_char_gain[0], word_squares), ("dp", "mp")
    )
    width = CHAR_BLOCK_WIDTH
    sum_mixer = jnp.stack(
        [sum_wide[:, t * width : (t + 1) * width] for t in range(3)] + [sum_out]
    )
    sum_lift = sum_lift[None]
    other_squares = (
        jnp.sum(sum_mixer * sum_mixer)
        + jnp.sum(sum_lift * sum_lift)
        + jnp.sum(sum_char_gain * sum_char_gain)
        + jnp.sum(sum_word_gains * sum_word_gains)
    )
    global_norm = jnp.sqrt(spread_squares / float(peer_count) + other_squares)
    parameter_count = (
        sum(
            part_count * w.size * peer_count
            for w in (word_project, word_output, feed_upper, feed_lower)
        )
        + peer_count * (char_mixer.size + char_lift.size)
        + char_gain.size
        + word_gains.size
    )
    factor = jnp.minimum(1.0, 0.5 * math.sqrt(parameter_count) / global_norm)
    mixer_root, lift_root, project_root, output_root, upper_root, lower_root = unpack(
        root_whole, [w.shape for w in roots]
    )
    mixer_out = refresh(char_mixer, sum_mixer, char_mixer_left, char_mixer_right, char_mixer_left_root, mixer_root, factor, owner_index)
    lift_out = refresh(char_lift, sum_lift, char_lift_left, char_lift_right, char_lift_left_root, lift_root, factor, owner_index)
    project_out = refresh(word_project, sum_project, word_project_left, word_project_right, word_project_left_root, project_root, factor, owner_index)
    output_out = refresh(word_output, sum_output, word_output_left, word_output_right, word_output_left_root, output_root, factor, owner_index)
    upper_out = refresh(feed_upper, sum_upper, feed_upper_left, feed_upper_right, feed_upper_left_root, upper_root, factor, owner_index)
    lower_out = refresh(feed_lower, sum_lower, feed_lower_left, feed_lower_right, feed_lower_left_root, lower_root, factor, owner_index)
    char_gain_clipped = factor * sum_char_gain
    word_gains_clipped = factor * sum_word_gains
    return (
        block_out,
        word_inputs_gradient,
        char_embeds_gradient,
        char_gain_clipped,
        word_gains_clipped,
        char_gain - gain_rate * char_gain_clipped,
        word_gains - gain_rate * word_gains_clipped,
        global_norm,
        mixer_out[0],
        mixer_out[1],
        mixer_out[2],
        mixer_out[3],
        mixer_out[4],
        lift_out[0],
        lift_out[1],
        lift_out[2],
        lift_out[3],
        lift_out[4],
        project_out[0],
        project_out[1],
        project_out[2],
        project_out[3],
        project_out[4],
        output_out[0],
        output_out[1],
        output_out[2],
        output_out[3],
        output_out[4],
        upper_out[0],
        upper_out[1],
        upper_out[2],
        upper_out[3],
        upper_out[4],
        lower_out[0],
        lower_out[1],
        lower_out[2],
        lower_out[3],
        lower_out[4],
    )


def solution(mesh):
    placed = (
        P("dp", None, None),
        P("dp", "mp", None, None),
        P("dp", None, None),
        P("dp", "mp"),
        P("dp", None),
        P("dp"),
        P("dp", None),
        P(),
        P(),
        P(None, "dp", None),
        P(None, "dp", None),
        P(None, "dp", None),
        P(None, "dp", None),
        P(None, "dp", None),
        P(None, "dp", None),
        P(None, "dp", None),
        P(None, "dp", None),
        P(None, "dp", None),
        P(None, "dp", None),
        P(None, "mp", "dp", None),
        P(None, "mp", "dp", None),
        P(None, "mp", "dp", None),
        P(None, "mp", "dp", None),
        P(None, "mp", "dp", None),
        P("mp", "dp", None),
        P("mp", "dp", None),
        P("mp", "dp", None),
        P("mp", "dp", None),
        P("mp", "dp", None),
        P("mp", "dp", None),
        P("mp", "dp", None),
        P("mp", "dp", None),
        P("mp", "dp", None),
        P("mp", "dp", None),
        P("mp", "dp", None),
        P("mp", "dp", None),
        P("mp", "dp", None),
        P("mp", "dp", None),
        P("mp", "dp", None),
    )
    return jax.shard_map(
        local,
        mesh=mesh,
        in_specs=placed,
        out_specs=(
            P("dp", None, None),
            P("dp", None, None),
            P("dp", "mp", None, None),
            P(),
            P(),
            P(),
            P(),
            P(),
            P(None, "dp", None),
            P(None, "dp", None),
            P(None, "dp", None),
            P(None, "dp", None),
            P(None, "dp", None),
            P(None, "dp", None),
            P(None, "dp", None),
            P(None, "dp", None),
            P(None, "dp", None),
            P(None, "dp", None),
            P(None, "mp", "dp", None),
            P(None, "mp", "dp", None),
            P(None, "mp", "dp", None),
            P(None, "mp", "dp", None),
            P(None, "mp", "dp", None),
            P("mp", "dp", None),
            P("mp", "dp", None),
            P("mp", "dp", None),
            P("mp", "dp", None),
            P("mp", "dp", None),
            P("mp", "dp", None),
            P("mp", "dp", None),
            P("mp", "dp", None),
            P("mp", "dp", None),
            P("mp", "dp", None),
            P("mp", "dp", None),
            P("mp", "dp", None),
            P("mp", "dp", None),
            P("mp", "dp", None),
            P("mp", "dp", None),
        ),
        check_vma=False,
    )
```

time: 1150 us -> 710 us (0.62)
  blocking collectives: 240 us -> 62.5 us
  local copies, waits for them, and re-layouts: 238 us -> 77.8 us
  matrix products: 220 us -> 86.4 us
  other arithmetic: 160 us -> 58.7 us
  Pallas kernels: 0 us -> 76.2 us
  waiting for transfers between devices: 248 us -> 303 us
    all_gather x12 -> x1, blocking collectives: 188 us -> 10.9 us  [local(): char_whole = lax.all_gather(char_pack, 'dp', axis=0, tiled=True)]
    dot_general x44 -> x29, matrix products: 186 us -> 47.6 us  [the longest x6 9.94 us: refresh(): jnp.matmul(half_step.astype(BF), right_root, preferred_element_type=F32)]
    pallas_call x0 -> x2, Pallas kernels: none -> 76.2 us  [the longest x1 44.9 us: char_backward(): pl.pallas_call(functools.partial(char_backward_kernel, classes), grid_spe...]
    squeeze x3 -> x0, local copies, waits for them, and re-layouts: 47.9 us -> none  [the longest x1 16 us: char_forward(): heads_view[0]]
    another operation x6 -> x4, local copies, waits for them, and re-layouts: 48.4 us -> 2.12 us  [the longest x1 1.16 us: local(): jnp.stack([sum_wide[:, t * width:(t + 1) * width] for t in range(3)] + [s...]
    convert_element_type x20 -> x12, other arithmetic: 47.7 us -> 11.5 us  [the longest x1 4.62 us: local(): grad_words = grad_stream.astype(BF)]
    psum x5, waiting for transfers between devices: 198 us -> 232 us  [the longest x1 72.3 us: local(): lax.psum((grad_wide, grad_out, grad_lift, grad_char_gain[0], word_squares...]
    sub x1 -> x3, other arithmetic: 28.5 us -> 0.01 us  [the longest x1 0.01 us: local(): jnp.max(jnp.where(to_slot[:, :, None], word_place[None] + 1, 0), axis=1) - 1]
  transfers between devices with their start and end apart: 9 -> 11, of which waited for: 6 -> 9; matrix products, arithmetic and copies ran while one was open for 6% -> 15% of each run, Pallas kernels for 0% -> 11%
where the time goes in v1:
time: 710 us; the launch traced here: 702 us
  waiting for transfers between devices  303 us (43%)
  matrix products  86.4 us (12%)
  local copies, waits for them, and re-layouts  77.8 us (11%)
  Pallas kernels  76.2 us (11%)
  blocking collectives  62.5 us (9%)
  other arithmetic  58.7 us (8%)
  between operations  22.6 us (3%)
  starting transfers between devices  14.4 us (2%)
    psum x1, waiting for transfers between devices, local(): lax.psum((grad_wide, grad_out, grad_lift, grad_char_gain[0], word_squares...  72.3 us
    psum x1, waiting for transfers between devices, local(): lax.psum(jnp.dot(active, lower_mats[0], preferred_element_type=F32).astyp...  58.1 us
    psum x1, waiting for transfers between devices, local(): lax.psum(jnp.dot(mixed_rows, output_mats[0], preferred_element_type=F32)....  49.8 us
    psum x1, waiting for transfers between devices, local(): grad_normed_two = lax.psum(part_two.astype(BF), 'mp').astype(F32)  45.2 us
    pallas_call x1, Pallas kernels, char_backward(): pl.pallas_call(functools.partial(char_backward_kernel, classes), grid_spe...  44.9 us
    psum x1, blocking collectives, local(): lax.psum((grad_wide, grad_out, grad_lift, grad_char_gain[0], word_squares...  39.6 us
    pallas_call x1, Pallas kernels, char_forward(): pl.pallas_call(functools.partial(char_forward_kernel, classes), grid_spec...  31.2 us
    unnamed x175, local copies, waits for them, and re-layouts  27.8 us
  transfers between devices with their start and end apart: 11, of which 9 were waited for; matrix products, arithmetic and copies ran while one was open for 15% of the time, Pallas kernels for 11%

profile of v1, /device:TPU:0, one launch (start us, length us, event | category | flops | bytes accessed | tf_op | source)
XLA Modules:
  0.0 701.7 jit_solution(16508591335787163566)
XLA Ops:
  11.3 5.2 all-to-all-start
  18.3 10.9 %all_gather.14.mats_ref = bf16[256,1536]{1,0:T(8,128)(2,1)S(1)} all-gather(bf16[32,1536]{1,0:T(8,128)(2,1)S(1)} %bitcast_dynamic-update-slice_fusion), channel_id=1, replica_groups=mesh['dp'=8,'mp'=4] {'dp'}, dimensions={0}, use_global_device_ids=true | all-gather | bytes 884736 | tf_op jit(solution)/shard_map/all_gather | solution.py:549
  32.4 31.2 %char_forward.1 = (bf16[640,512]{1,0:T(8,128)(2,1)S(1)}, bf16[20,512,1536]{2,1,0:T(8,128)(2,1)}, bf16[640,256]{1,0:T(8,128)(2,1)S(1)}, f32[640,256]{1,0:T(8,128)S(1)}) custom-call(s32[20]{0:T(128)S(1)} %get-tuple-element.357.kind, bf16[20,512,256]{2,1,0:T(8,128)(2,1)S(1)} %bitcast.444, f32[20,32,128]{2,1,0:T(8,128)S(1)} %broadcast_in_dim.207.count_ref, ...), custom_call_target="tpu_custom_call" | custom-call | flops 10737418240 | bytes 47185920 | tf_op jit(solution)/shard_map/char_forward/pallas_call | solution.py:155
  67.6 3.5 all-to-all-start.1
  72.1 11.6 %all-to-all-done.1 = bf16[24,32,512]{2,1,0:T(8,128)(2,1)S(1)} async-done(((bf16[24,32,512]{2,1,0:T(8,128)(2,1)}), bf16[24,32,512]{2,1,0:T(8,128)(2,1)S(1)}, u32[]{:S(2)}, u32[]{:S(2)}) %all-to-all-start.1) | async-done | bytes 786464 | tf_op jit(solution)/shard_map/all_to_all | solution.py:607
  101.9 15.8 %all-gather.4.cloned.1.call-done = bf16[4,320,512]{2,1,0:T(8,128)(2,1)} async-done(((bf16[1,320,512]{2,1,0:T(8,128)(2,1)}), bf16[4,320,512]{2,1,0:T(8,128)(2,1)}) %all-gather.4.cloned.1.call-update) | async-done | bytes 1310736 | tf_op jit(solution)/shard_map/all_gather | solution.py:613
  117.7 4.6 multiply_reduce_fusion.3
  122.9 21.9 %all-gather.6.cloned.1.call-done = bf16[8,768,128]{2,1,0:T(8,128)(2,1)} async-done(((bf16[1,768,128]{2,1,0:T(8,128)(2,1)}), bf16[8,768,128]{2,1,0:T(8,128)(2,1)}) %all-gather.6.cloned.1.call-update) | async-done | bytes 1572880 | tf_op jit(solution)/shard_map/all_gather | solution.py:550
  149.9 4.8 fusion.217
  154.7 3.6 fusion.218
  167.0 49.8 %all-reduce.10.cloned.1.call-done = bf16[1024,512]{0,1:T(8,128)(2,1)} async-done(((bf16[1024,512]{0,1:T(8,128)(2,1)}), bf16[1024,512]{0,1:T(8,128)(2,1)}) %all-reduce.10.cloned.1.call-update) | async-done | bytes 1048592 | tf_op jit(solution)/shard_map/psum | solution.py:634
  228.1 3.6 convolution_convert_fusion.5
  231.7 45.2 %all-reduce.12.cloned.1.call-done = bf16[1024,512]{0,1:T(8,128)(2,1)} async-done(((bf16[1024,512]{0,1:T(8,128)(2,1)}), bf16[1024,512]{0,1:T(8,128)(2,1)}) %all-reduce.12.cloned.1.call-update) | async-done | bytes 1048592 | tf_op jit(solution)/shard_map/psum | solution.py:654
  294.6 4.1 multiply_convert_fusion
  334.7 3.6 fusion.41
  340.0 58.1 %all-reduce.18.cloned.1.call-done = (bf16[1024,512]{0,1:T(8,128)(2,1)}, bf16[1024,512]{0,1:T(8,128)(2,1)}) async-done(((bf16[1024,512]{0,1:T(8,128)(2,1)}, bf16[1024,512]{0,1:T(8,128)(2,1)}), (bf16[1024,512]{0,1:T(8,128)(2,1)}, bf16[1024,512]{0,1:T(8,128)(2,1)})) %all-reduce.18.cloned.1.call-update) | async-done | bytes 2097168 | tf_op jit(solution)/shard_map/psum | solution.py:642
  400.9 4.6 fusion.13
  407.5 4.2 all-to-all-start.2
  411.7 21.4 %all-gather.8.cloned.1.call-done = bf16[8,1328,128]{2,1,0:T(8,128)(2,1)} async-done(((bf16[1,1328,128]{2,1,0:T(8,128)(2,1)}), bf16[8,1328,128]{2,1,0:T(8,128)(2,1)}) %all-gather.8.cloned.1.call-update) | async-done | bytes 2719760 | tf_op jit(solution)/shard_map/all_gather | solution.py:566
  457.1 44.9 %char_backward.1 = (bf16[20,512,256]{2,1,0:T(8,128)(2,1)}, f32[256,768]{1,0:T(8,128)}, f32[256,256]{1,0:T(8,128)}, f32[256,512]{1,0:T(8,128)}, f32[1,256]{1,0:T(1,128)S(1)}) custom-call(s32[20]{0:T(128)S(1)} %get-tuple-element.357.kind, bf16[20,512,256]{2,1,0:T(8,128)(2,1)S(1)} %bitcast.445, f32[20,32,128]{2,1,0:T(8,128)S(1)} %broadcast_in_dim.207.count_ref, ...), custom_call_target="tpu_custom_call" | custom-call | flops 18790481920 | bytes 47185920 | tf_op jit(solution)/shard_map/char_backward/pallas_call | solution.py:286
  502.1 6.9 all-reduce.16.cloned.1.call-done
  521.5 12.0 %psum.111 = bf16[2,512]{1,0:T(2,128)(2,1)S(1)} all-reduce(bf16[2,512]{1,0:T(2,128)(2,1)S(1)} %pad_maximum_fusion.6), channel_id=1, replica_groups=mesh['dp'=8,'mp'=4] {'dp'}, use_global_device_ids=true, to_apply=%region_38.39 | all-reduce | flops 1024 | bytes 4096 | tf_op jit(solution)/shard_map/psum | solution.py:704
  534.1 39.6 %all-reduce = (f32[256]{0:T(256)S(1)}, f32[]{:T(128)}) all-reduce(f32[256]{0:T(256)S(1)} %bitcast.446, f32[]{:T(128)S(6)} %add.300), channel_id=1, replica_groups=mesh['dp'=8,'mp'=4] {'dp','mp'}, use_global_device_ids=true, to_apply=%region_34.35 | all-reduce | flops 257 | bytes 2056 | tf_op jit(solution)/shard_map/psum | solution.py:721
  575.0 72.3 %all-reduce.14.cloned.1.call-done = (f32[1,256,256]{2,1,0:T(8,128)}, f32[256,768]{1,0:T(8,128)}, f32[256,512]{1,0:T(8,128)}) async-done(((f32[1,256,256]{2,1,0:T(8,128)}, f32[256,768]{1,0:T(8,128)}, f32[256,512]{1,0:T(8,128)}), (f32[1,256,256]{2,1,0:T(8,128)}, f32[256,768]{1,0:T(8,128)}, f32[256,512]{1,0:T(8,128)})) %all-reduce.14.cloned.1.call-update) | async-done | bytes 1572880 | tf_op jit(solution)/shard_map/psum | solution.py:721
  (372 shorter events, 195.5 us)
Async XLA Ops:
  7.2 22.7 %copy-start = (f32[256]{0:T(256)S(1)}, f32[256]{0:T(256)}, u32[]{:S(2)}) copy-start(f32[256]{0:T(256)} %param.46) | copy-start | bytes 3076
  10.4 54.5 %copy-start.70 = (s32[20]{0:T(128)}, s32[20]{0:T(128)S(1)}, u32[]{:S(2)}) copy-start(s32[20]{0:T(128)S(1)} %get-tuple-element.356) | copy-start | bytes 244
  11.3 56.4 %all-to-all-start = ((s32[8,3,128]{2,1,0:T(4,128)}), s32[8,3,128]{2,1,0:T(4,128)S(1)}, u32[]{:S(2)}, u32[]{:S(2)}) async-start(s32[8,3,128]{2,1,0:T(4,128)} %sub.143), calls=%async_computation | async-start | bytes 32768 | tf_op jit(solution)/shard_map/all_to_all | solution.py:592
  67.6 16.1 %all-to-all-start.1 = ((bf16[24,32,512]{2,1,0:T(8,128)(2,1)}), bf16[24,32,512]{2,1,0:T(8,128)(2,1)S(1)}, u32[]{:S(2)}, u32[]{:S(2)}) async-start(bf16[24,32,512]{2,1,0:T(8,128)(2,1)} %bitcast.144), calls=%async_computation.1 | async-start | bytes 1572864 | tf_op jit(solution)/shard_map/all_to_all | solution.py:607
  71.2 46.5 %all-gather.4.cloned.1.call-start = ((), (), s32[]{:S(2)}) async-start(), calls=%async_computation.3 | async-start | bytes 1638400 | tf_op jit(solution)/shard_map/all_gather | solution.py:613
  72.1 19.0 %copy-start.78 = (s32[24]{0:T(128)}, s32[24]{0:T(128)S(1)}, u32[]{:S(2)}) copy-start(s32[24]{0:T(128)S(1)} %broadcast_select_fusion) | copy-start | bytes 292
  85.5 59.4 %all-gather.6.cloned.1.call-start = ((), (), s32[]{:S(2)}) async-start(), calls=%async_computation.4 | async-start | bytes 1769472 | tf_op jit(solution)/shard_map/all_gather | solution.py:550
  95.8 121.0 %all-reduce.10.cloned.1.call-start = ((), (), s32[]{:S(2)}) async-start(), calls=%async_computation.5 | async-start | bytes 2097152 | tf_op jit(solution)/shard_map/psum | solution.py:634
  98.4 47.5 %copy-start.61 = (f32[1,512]{1,0:T(1,128)}, f32[1,512]{1,0:T(1,128)S(1)}, u32[]{:S(2)}) copy-start(f32[1,512]{1,0:T(1,128)S(1)} %get-tuple-element.351) | copy-start | bytes 6148
  164.9 112.1 %all-reduce.12.cloned.1.call-start = ((), (), s32[]{:S(2)}) async-start(), calls=%async_computation.6 | async-start | bytes 2097152 | tf_op jit(solution)/shard_map/psum | solution.py:654
  225.6 172.5 %all-reduce.18.cloned.1.call-start = ((), (), s32[]{:S(2)}) async-start(), calls=%async_computation.10 | async-start | bytes 4194304 | tf_op jit(solution)/shard_map/psum | solution.py:642
  311.5 121.7 %all-gather.8.cloned.1.call-start = ((), (), s32[]{:S(2)}) async-start(), calls=%async_computation.7 | async-start | bytes 3059712 | tf_op jit(solution)/shard_map/all_gather | solution.py:566
  338.3 59.8 %copy-start.62 = (f32[1,512]{1,0:T(1,128)S(1)}, f32[1,512]{1,0:T(1,128)}, u32[]{:S(2)}) copy-start(f32[1,512]{1,0:T(1,128)} %copy-done.61) | copy-start | bytes 6148
  340.0 60.9 %copy-start.57 = (f32[1024]{0:T(1024)S(1)}, f32[1024]{0:T(1024)}, u32[]{:S(2)}) copy-start(f32[1024]{0:T(1024)} %get-tuple-element.348) | copy-start | bytes 12292
  340.0 60.9 %copy-start.59 = (f32[1024]{0:T(1024)S(1)}, f32[1024]{0:T(1024)}, u32[]{:S(2)}) copy-start(f32[1024]{0:T(1024)} %copy-done.58) | copy-start | bytes 12292
  340.0 60.9 %copy-start.65 = (f32[1024]{0:T(1024)S(1)}, f32[1024]{0:T(1024)}, u32[]{:S(2)}) copy-start(f32[1024]{0:T(1024)} %get-tuple-element.346) | copy-start | bytes 12292
  407.5 42.3 %all-to-all-start.2 = ((bf16[24,32,512]{2,1,0:T(8,128)(2,1)}), bf16[24,32,512]{2,1,0:T(8,128)(2,1)}, u32[]{:S(2)}, u32[]{:S(2)}) async-start(bf16[24,32,512]{2,1,0:T(8,128)(2,1)} %bitcast.479), calls=%async_computation.2 | async-start | bytes 1572864 | tf_op jit(solution)/shard_map/all_to_all | solution.py:691
  411.7 97.3 %all-reduce.16.cloned.1.call-start = ((), (), s32[]{:S(2)}) async-start(), calls=%async_computation.9 | async-start | bytes 3145728 | tf_op jit(solution)/shard_map/psum | solution.py:704
  449.5 197.8 %all-reduce.14.cloned.1.call-start = ((), (), s32[]{:S(2)}) async-start(), calls=%async_computation.8 | async-start | bytes 3145728 | tf_op jit(solution)/shard_map/psum | solution.py:721
  502.0 16.8 %copy-start.14 = (bf16[1,1024,512]{1,2,0:T(8,128)(2,1)S(1)}, bf16[1,1024,512]{1,2,0:T(8,128)(2,1)}, u32[]{:S(2)}) copy-start(bf16[1,1024,512]{1,2,0:T(8,128)(2,1)} %get-tuple-element.322) | copy-start | bytes 3145732
  502.1 18.1 %copy-start.13 = (bf16[1024,512]{0,1:T(8,128)(2,1)S(1)}, bf16[1024,512]{0,1:T(8,128)(2,1)}, u32[]{:S(2)}) copy-start(bf16[1024,512]{0,1:T(8,128)(2,1)} %copy-done.12) | copy-start | bytes 3145732
  521.5 132.9 %copy-start.67 = (f32[2,512]{1,0:T(2,128)S(1)}, f32[2,512]{1,0:T(2,128)}, u32[]{:S(2)}) copy-start(f32[2,512]{1,0:T(2,128)} %param.47) | copy-start | bytes 12292
  521.5 133.5 %copy-start.38 = (bf16[1,128,512]{2,1,0:T(8,128)(2,1)S(1)}, bf16[1,128,512]{2,1,0:T(8,128)(2,1)}, u32[]{:S(2)}) copy-start(bf16[1,128,512]{2,1,0:T(8,128)(2,1)} %get-tuple-element.301) | copy-start | bytes 393220
  665.4 14.1 %copy-start.27 = (bf16[8,1,4,64,128]{4,2,3,0,1:T(4,128)(2,1)S(1)}, bf16[8,1,4,64,128]{4,2,3,0,1:T(4,128)(2,1)}, u32[]{:S(2)}) copy-start(bf16[8,1,4,64,128]{4,2,3,0,1:T(4,128)(2,1)} %copy.273) | copy-start | bytes 1572868
  (68 other events, 305.3 us)
Sparse Core Ops, SparseCore 0:
  85.6 32.0 all-gather.3
  120.1 24.6 all-gather.5
  165.0 51.8 all-reduce.9
  225.7 51.1 all-reduce.11
  311.6 86.4 all-reduce.17
  400.5 32.5 all-gather.7
  449.6 59.3 all-reduce.15
  514.7 132.5 all-reduce.13

commit v2 on v1

--- a/solution.py
+++ b/solution.py
@@ -448,6 +448,180 @@
     return lax.map(one_row, (queries, keys_all, values_all, grad_mixed, documents))
 
 
+MESH_ID = pl.DeviceIdType.MESH
+
+
+def exchange(name, number, tasks):
+    sizes = {axis: lax.axis_size(axis) for _, axis, _ in tasks}
+    outs, scratch = [], []
+    for kind, axis, array in tasks:
+        n = sizes[axis]
+        block = array.shape if kind == "gather" else array.shape[1:]
+        outs.append(
+            jax.ShapeDtypeStruct(
+                block if kind == "part" else (n,) + block, F32 if kind == "part" else array.dtype
+            )
+        )
+        scratch += [pltpu.SemaphoreType.DMA((2, n)), pltpu.SemaphoreType.DMA((2, n))]
+        if kind in ("part", "sum"):
+            scratch.append(pltpu.VMEM((n,) + block, array.dtype))
+
+    def kernel(*refs):
+        ins, results = refs[: len(tasks)], refs[len(tasks) : 2 * len(tasks)]
+        rest = list(refs[2 * len(tasks) :])
+        me = {axis: lax.axis_index(axis) for axis in sizes}
+        barrier = pltpu.get_barrier_semaphore()
+        for axis, n in sizes.items():
+            for d in range(1, n):
+                pl.semaphore_signal(
+                    barrier, inc=1, device_id={axis: lax.rem(me[axis] + d, n)}, device_id_type=MESH_ID
+                )
+        pl.semaphore_wait(barrier, sum(n - 1 for n in sizes.values()))
+
+        def send(axis, source, target, sems, phase):
+            n = sizes[axis]
+            copies = []
+            for d in range(1, n):
+                peer = lax.rem(me[axis] + d, n)
+                copies.append(
+                    pltpu.make_async_remote_copy(
+                        src_ref=source(peer),
+                        dst_ref=target.at[me[axis]],
+                        send_sem=sems[0].at[phase, d],
+                        recv_sem=sems[1].at[phase, d],
+                        device_id={axis: peer},
+                        device_id_type=MESH_ID,
+                    )
+                )
+            for copy in copies:
+                copy.start()
+            return copies
+
+        plans = []
+        for (kind, axis, _), x, out in zip(tasks, ins, results):
+            sems = (rest.pop(0), rest.pop(0))
+            held = rest.pop(0) if kind in ("part", "sum") else out
+            source = (lambda p, x=x: x) if kind == "gather" else (lambda p, x=x: x.at[p])
+            plans.append((kind, axis, x, out, sems, held, send(axis, source, held, sems, 0)))
+        for kind, axis, x, out, sems, held, copies in plans:
+            held[me[axis]] = x[...] if kind == "gather" else x[me[axis]]
+        waiting = []
+        for kind, axis, x, out, sems, held, copies in plans:
+            if kind in ("gather", "swap"):
+                waiting += copies
+                continue
+            for copy in copies:
+                copy.wait()
+            total = held[0].astype(F32)
+            for p in range(1, sizes[axis]):
+                total = total + held[p].astype(F32)
+            if kind == "part":
+                out[...] = total
+            else:
+                out[me[axis]] = total.astype(out.dtype)
+                waiting += send(axis, lambda p, out=out, axis=axis: out.at[me[axis]], out, sems, 1)
+        for copy in waiting:
+            copy.wait()
+
+    vmem = pl.BlockSpec(memory_space=pltpu.VMEM)
+    return pl.pallas_call(
+        kernel,
+        out_shape=outs,
+        in_specs=[vmem] * len(tasks),
+        out_specs=[vmem] * len(tasks),
+        scratch_shapes=scratch,
+        compiler_params=pltpu.CompilerParams(
+            collective_id=number, has_side_effects=True, vmem_limit_bytes=48 << 20
+        ),
+        name=name,
+    )(*[array for _, _, array in tasks])
+
+
+def sum_char_grads(grads, small):
+    n, m = lax.axis_size("dp"), lax.axis_size("mp")
+    block = grads.shape[1:]
+
+    def kernel(x, s, out, small_out, held, held_z, small_dp, small_mp, ss, rs):
+        i, j = lax.axis_index("dp"), lax.axis_index("mp")
+        barrier = pltpu.get_barrier_semaphore()
+        for d in range(1, n):
+            pl.semaphore_signal(barrier, inc=1, device_id={"dp": lax.rem(i + d, n)}, device_id_type=MESH_ID)
+        for d in range(1, m):
+            pl.semaphore_signal(barrier, inc=1, device_id={"mp": lax.rem(j + d, m)}, device_id_type=MESH_ID)
+        pl.semaphore_wait(barrier, n + m - 2)
+
+        def send(axis, me, count, source, target, phase):
+            copies = []
+            for d in range(1, count):
+                peer = lax.rem(me + d, count)
+                copies.append(
+                    pltpu.make_async_remote_copy(
+                        src_ref=source(peer), dst_ref=target.at[me], send_sem=ss.at[phase, d],
+                        recv_sem=rs.at[phase, d], device_id={axis: peer}, device_id_type=MESH_ID,
+                    )
+                )
+            for copy in copies:
+                copy.start()
+            return copies
+
+        small_one = send("dp", i, n, lambda p: s, small_dp, 0)
+        one = send("dp", i, n, lambda p: x.at[p], held, 1)
+        held[i] = x[i]
+        small_dp[i] = s[...]
+        for copy in small_one:
+            copy.wait()
+        total = small_dp[0]
+        for p in range(1, n):
+            total = total + small_dp[p]
+        small_mp[j] = total
+        small_two = send("mp", j, m, lambda p: small_mp.at[j], small_mp, 2)
+        for copy in one:
+            copy.wait()
+        total = held[0].astype(F32)
+        for p in range(1, n):
+            total = total + held[p].astype(F32)
+        held_z[j] = total.astype(BF)
+        two = send("mp", j, m, lambda p: held_z.at[j], held_z, 3)
+        for copy in small_two:
+            copy.wait()
+        total = small_mp[0]
+        for p in range(1, m):
+            total = total + small_mp[p]
+        small_out[...] = total
+        for copy in two:
+            copy.wait()
+        total = held_z[0].astype(F32)
+        for p in range(1, m):
+            total = total + held_z[p].astype(F32)
+        out[i] = total.astype(BF)
+        three = send("dp", i, n, lambda p: out.at[i], out, 4)
+        for copy in three:
+            copy.wait()
+
+    vmem = pl.BlockSpec(memory_space=pltpu.VMEM)
+    return pl.pallas_call(
+        kernel,
+        out_shape=[
+            jax.ShapeDtypeStruct(grads.shape, BF),
+            jax.ShapeDtypeStruct(small.shape, F32),
+        ],
+        in_specs=[vmem] * 2,
+        out_specs=[vmem] * 2,
+        scratch_shapes=[
+            pltpu.VMEM((n,) + block, BF),
+            pltpu.VMEM((m,) + block, BF),
+            pltpu.VMEM((n,) + small.shape, F32),
+            pltpu.VMEM((m,) + small.shape, F32),
+            pltpu.SemaphoreType.DMA((5, max(n, m))),
+            pltpu.SemaphoreType.DMA((5, max(n, m))),
+        ],
+        compiler_params=pltpu.CompilerParams(
+            collective_id=20, has_side_effects=True, vmem_limit_bytes=48 << 20
+        ),
+        name="sum_char_grads",
+    )(grads, small)
+
+
 def pack(array):
     rows, cols = array.shape[-2:]
     if cols % 128:
@@ -546,15 +720,7 @@
     char_pack = jnp.concatenate(
         [char_mixer[0], char_mixer[1], char_mixer[2], char_mixer[3], char_lift[0]], axis=1
     ).astype(BF)
-    char_whole = lax.all_gather(char_pack, "dp", axis=0, tiled=True)
-    word_whole = lax.all_gather(
-        jnp.concatenate([pack(w) for w in (word_project, word_output, feed_upper, feed_lower)]).astype(BF),
-        "dp",
-        axis=0,
-    )
-    project_mats, output_mats, upper_mats, lower_mats = unpack(
-        word_whole, [w.shape for w in (word_project, word_output, feed_upper, feed_lower)]
-    )
+    word_masters = (word_project, word_output, feed_upper, feed_lower)
     roots = (
         char_mixer_right_root,
         char_lift_right_root,
@@ -563,10 +729,6 @@
         feed_upper_right_root,
         feed_lower_right_root,
     )
-    root_whole = lax.all_gather(
-        jnp.concatenate([pack(w) for w in roots]).astype(BF), "dp", axis=0
-    )
-
     peers = lax.broadcasted_iota(jnp.int32, (slot_count, peer_count), 1)
     owner_match = (block_home[:, None] == peers).astype(jnp.int32)
     earlier = (
@@ -578,6 +740,19 @@
     slot_target = jnp.where(block_home >= 0, block_home * pair_cap + slot_rank, slot_total)
     to_slot = lax.broadcasted_iota(jnp.int32, (slot_total, slot_count), 0) == slot_target[None, :]
 
+    sent_place = jnp.max(
+        jnp.where(to_slot[:, :, None], word_place[None] + 1, 0), axis=1
+    ) - 1
+    gathered, came_place = exchange(
+        "gather_char",
+        0,
+        [
+            ("gather", "dp", char_pack),
+            ("swap", "dp", sent_place.reshape(peer_count, pair_cap, block_words)),
+        ],
+    )
+    char_whole = gathered.reshape(-1, char_pack.shape[1])
+    came_place = came_place.reshape(slot_total, block_words)
     kind = char_kind(block_home, char_count, share_rows)
     counts = jnp.broadcast_to(
         char_count.astype(F32)[..., None], (slot_count, share_rows, 128)
@@ -586,10 +761,6 @@
         character_embeddings, kind, counts, char_gain, char_whole
     )
 
-    sent_place = jnp.max(
-        jnp.where(to_slot[:, :, None], word_place[None] + 1, 0), axis=1
-    ) - 1
-    came_place = lax.all_to_all(sent_place, "dp", split_axis=0, concat_axis=0, tiled=True)
     live = jnp.max(came_place, axis=1) >= 0
     slots_before = (
         lax.broadcasted_iota(jnp.int32, (slot_total, slot_total), 1)
@@ -604,13 +775,23 @@
     sent = jnp.dot(
         to_slot.astype(BF), word_vectors.reshape(slot_count, wide), preferred_element_type=F32
     ).astype(BF)
-    came = lax.all_to_all(
-        sent.reshape(slot_total, share_rows, D), "dp", split_axis=0, concat_axis=0, tiled=True
+    (came,) = exchange(
+        "send_vectors", 1, [("swap", "dp", sent.reshape(peer_count, pair_cap * share_rows, D))]
     )
     compact = jnp.dot(
         to_live.astype(BF), came.reshape(slot_total, wide), preferred_element_type=F32
     ).astype(BF)
-    live_vectors = lax.all_gather(compact.reshape(OWNER_BLOCKS * share_rows, D), "mp", axis=0)
+    live_vectors, word_whole = exchange(
+        "gather_words",
+        2,
+        [
+            ("gather", "mp", compact.reshape(OWNER_BLOCKS * share_rows, D)),
+            ("gather", "dp", jnp.concatenate([pack(w) for w in word_masters]).astype(BF)),
+        ],
+    )
+    project_mats, output_mats, upper_mats, lower_mats = unpack(
+        word_whole, [w.shape for w in word_masters]
+    )
     place_parts = live_place.reshape(OWNER_BLOCKS, part_count, share_rows)
     place_flat = place_parts.transpose(1, 0, 2).reshape(-1)
     numbers = lax.broadcasted_iota(jnp.int32, (words_dev, place_flat.shape[0]), 0)
@@ -631,18 +812,22 @@
     mixed_rows = word_attention(heads_view[0], heads_view[1], heads_view[2], documents).reshape(
         words_dev, block_width
     )
-    attend_total = lax.psum(
-        jnp.dot(mixed_rows, output_mats[0], preferred_element_type=F32).astype(BF), "mp"
-    ).astype(F32)
-    hidden = stream + attend_total
+    shares = (part_count, words_dev // part_count, D)
+    attend_part = jnp.dot(mixed_rows, output_mats[0], preferred_element_type=F32).astype(BF)
+    attend_total, root_whole = exchange(
+        "sum_attend",
+        3,
+        [
+            ("sum", "mp", attend_part.reshape(shares)),
+            ("gather", "dp", jnp.concatenate([pack(w) for w in roots]).astype(BF)),
+        ],
+    )
+    hidden = stream + attend_total.reshape(words_dev, D).astype(F32)
     normed_float_two, scale_two = norm_forward(hidden, word_gains[1])
     normed_two = normed_float_two.astype(BF)
     upper_rows = jnp.dot(normed_two, upper_mats[0], preferred_element_type=F32)
     active = gelu_tanh(upper_rows).astype(BF)
-    feed_total = lax.psum(
-        jnp.dot(active, lower_mats[0], preferred_element_type=F32).astype(BF), "mp"
-    ).astype(F32)
-    block_out = (hidden + feed_total).astype(BF).reshape(word_inputs.shape)
+    feed_part = jnp.dot(active, lower_mats[0], preferred_element_type=F32).astype(BF)
     grad_output = cotangent.reshape(words_dev, D).astype(F32)
     grad_feed = grad_output.astype(BF)
     grad_lower = jnp.einsum("rf,rd->fd", active, grad_feed, preferred_element_type=F32)
@@ -651,7 +836,10 @@
     grad_upper_rows = gelu_pull(grad_active)[0].astype(BF)
     grad_upper = jnp.einsum("rd,rf->df", normed_two, grad_upper_rows, preferred_element_type=F32)
     part_two = jnp.einsum("rf,df->rd", grad_upper_rows, upper_mats[0], preferred_element_type=F32)
-    grad_normed_two = lax.psum(part_two.astype(BF), "mp").astype(F32)
+    (grad_normed_two,) = exchange(
+        "sum_part_two", 4, [("sum", "mp", part_two.astype(BF).reshape(shares))]
+    )
+    grad_normed_two = grad_normed_two.reshape(words_dev, D).astype(F32)
     grad_hidden_norm, gain_two = norm_backward(hidden, scale_two, word_gains[1], grad_normed_two)
     grad_hidden = grad_output + grad_hidden_norm
     grad_attend = grad_hidden.astype(BF)
@@ -671,7 +859,23 @@
     part_one = jnp.einsum(
         "tre,tde->rd", grad_heads, project_mats[:, 0], preferred_element_type=F32
     )
-    grad_normed_one = lax.psum(part_one.astype(BF), "mp").astype(F32)
+    word_grads = [
+        jnp.moveaxis(
+            g.astype(BF).reshape(g.shape[:-2] + (peer_count, -1, g.shape[-1])), -3, 0
+        )
+        for g in (grad_project, grad_output_mat, grad_upper, grad_lower)
+    ]
+    grad_normed_one, *word_sums = exchange(
+        "sum_part_one",
+        5,
+        [("sum", "mp", part_one.astype(BF).reshape(shares))]
+        + [("sum", "dp", g) for g in word_grads],
+    )
+    grad_normed_one = grad_normed_one.reshape(words_dev, D).astype(F32)
+    sum_project, sum_output, sum_upper, sum_lower = (
+        jnp.moveaxis(g, 0, -3).reshape(w.shape[:-2] + (-1, w.shape[-1])).astype(F32)
+        for g, w in zip(word_sums, word_masters)
+    )
     grad_stream_norm, gain_one = norm_backward(stream, scale_one, word_gains[0], grad_normed_one)
     grad_stream = grad_hidden + grad_stream_norm
     grad_words = grad_stream.astype(BF)
@@ -688,29 +892,19 @@
         grad_words,
         preferred_element_type=F32,
     ).astype(BF)
-    returned = lax.all_to_all(
-        picked.reshape(slot_total, share_rows, D), "dp", split_axis=0, concat_axis=0, tiled=True
+    (returned,) = exchange(
+        "return_vectors", 6, [("swap", "dp", picked.reshape(peer_count, pair_cap * share_rows, D))]
     )
     grad_vectors = (
         jnp.dot(to_slot.astype(BF).T, returned.reshape(slot_total, wide), preferred_element_type=F32)
         .astype(BF)
         .reshape(slot_count * share_rows, D)
     )
+    grad_vectors, feed_part = lax.optimization_barrier((grad_vectors, feed_part))
+    feed_total = lax.psum(feed_part, "mp").astype(F32)
+    block_out = (hidden + feed_total).astype(BF).reshape(word_inputs.shape)
     char_embeds_gradient, grad_wide, grad_out, grad_lift, grad_char_gain = char_backward(
         character_embeddings, kind, counts, char_gain, char_whole, kept, pooled, msum, grad_vectors
-    )
-    sum_project, sum_output, sum_upper, sum_lower, sum_word_gains = (
-        s.astype(F32)
-        for s in lax.psum(
-            (
-                grad_project[:, None].astype(BF),
-                grad_output_mat[None].astype(BF),
-                grad_upper[None].astype(BF),
-                grad_lower[None].astype(BF),
-                jnp.stack([gain_one, gain_two]).astype(BF),
-            ),
-            "dp",
-        )
     )
     word_squares = (
         jnp.sum(sum_project * sum_project)
@@ -718,21 +912,26 @@
         + jnp.sum(sum_upper * sum_upper)
         + jnp.sum(sum_lower * sum_lower)
     )
-    sum_wide, sum_out, sum_lift, sum_char_gain, spread_squares = lax.psum(
-        (grad_wide, grad_out, grad_lift, grad_char_gain[0], word_squares), ("dp", "mp")
-    )
     width = CHAR_BLOCK_WIDTH
-    sum_mixer = jnp.stack(
-        [sum_wide[:, t * width : (t + 1) * width] for t in range(3)] + [sum_out]
-    )
-    sum_lift = sum_lift[None]
+    small = jnp.zeros((8, D), F32)
+    small = small.at[0, :width].set(grad_char_gain[0])
+    small = small.at[1:3].set(jnp.stack([gain_one, gain_two]) / part_count)
+    small = small.at[3, 0].set(word_squares / peer_count)
+    char_grads = jnp.concatenate([grad_wide, grad_out, grad_lift], axis=1).astype(BF)
+    char_sums, small_sums = sum_char_grads(
+        char_grads.reshape(peer_count, -1, char_grads.shape[1]), small
+    )
+    char_sums = char_sums.reshape(char_grads.shape).astype(F32)
+    sum_mixer = jnp.stack([char_sums[:, t * width : (t + 1) * width] for t in range(4)])
+    sum_lift = char_sums[None, :, 4 * width :]
+    sum_char_gain, sum_word_gains = small_sums[0, :width], small_sums[1:3]
     other_squares = (
         jnp.sum(sum_mixer * sum_mixer)
         + jnp.sum(sum_lift * sum_lift)
         + jnp.sum(sum_char_gain * sum_char_gain)
         + jnp.sum(sum_word_gains * sum_word_gains)
     )
-    global_norm = jnp.sqrt(spread_squares / float(peer_count) + other_squares)
+    global_norm = jnp.sqrt(small_sums[3, 0] + other_squares)
     parameter_count = (
         sum(
             part_count * w.size * peer_count

time: 710 us -> 565 us (0.80)
  waiting for transfers between devices: 303 us -> 0.02 us
  Pallas kernels: 76.2 us -> 322 us
  blocking collectives: 62.5 us -> 0 us
  starting transfers between devices: 14.4 us -> 0.04 us
  matrix products: 86.4 us -> 79.3 us
    pallas_call x0 -> x8, Pallas kernels: none -> 278 us  [the longest x7 227 us: exchange(): pl.pallas_call(kernel, out_shape=outs, in_specs=[vmem] * len(tasks), out_...]
    psum x5 -> x1, waiting for transfers between devices: 232 us -> 0.01 us  [local(): feed_total = lax.psum(feed_part, 'mp').astype(F32)]
    all_gather x3 -> x0, waiting for transfers between devices: 59.1 us -> none  [the longest x1 21.9 us: local(): lax.all_gather(jnp.concatenate([pack(w) for w in (word_project, word_outp...]
    psum x2 -> x0, blocking collectives: 51.6 us -> none  [the longest x1 39.6 us: local(): lax.psum((grad_wide, grad_out, grad_lift, grad_char_gain[0], word_squares...]
    pallas_call x1, Pallas kernels: 44.9 us -> 26.1 us  [char_backward(): pl.pallas_call(functools.partial(char_backward_kernel, classes), grid_spe...]
    all_to_all x3 -> x0, starting transfers between devices: 12.9 us -> none  [the longest x1 5.17 us: local(): lax.all_to_all(sent_place, 'dp', split_axis=0, concat_axis=0, tiled=True)]
    pallas_call x1, Pallas kernels: 31.2 us -> 18.3 us  [char_forward(): pl.pallas_call(functools.partial(char_forward_kernel, classes), grid_spec...]
    convert_element_type x0 -> x5, local copies, waits for them, and re-layouts: none -> 12 us  [the longest x1 3.32 us: local(): grad_normed_one = grad_normed_one.reshape(words_dev, D).astype(F32)]
  transfers between devices with their start and end apart: 11 -> 1, of which waited for: 9 -> 0; matrix products, arithmetic and copies ran while one was open for 15% -> 12% of each run, Pallas kernels for 11% -> 14%
where the time goes in v2:
time: 565 us; the launch traced here: 560 us
  Pallas kernels  322 us (57%)
  matrix products  79.3 us (14%)
  local copies, waits for them, and re-layouts  71.4 us (13%)
  other arithmetic  63.8 us (11%)
  between operations  22.9 us (4%)
    pallas_call x7, Pallas kernels, exchange(): pl.pallas_call(kernel, out_shape=outs, in_specs=[vmem] * len(tasks), out_...  227 us
    pallas_call x1, Pallas kernels, sum_char_grads(): pl.pallas_call(kernel, out_shape=[jax.ShapeDtypeStruct(grads.shape, BF),...  51.2 us
    unnamed x246, local copies, waits for them, and re-layouts  26.6 us
    pallas_call x1, Pallas kernels, char_backward(): pl.pallas_call(functools.partial(char_backward_kernel, classes), grid_spe...  26.1 us
    pallas_call x1, Pallas kernels, char_forward(): pl.pallas_call(functools.partial(char_forward_kernel, classes), grid_spec...  18.3 us
    and x1, other arithmetic, word_softmax(): allowed = (key_at <= query_at) & (key_docs[None, :] == query_docs[:, None])  12 us
    dot_general x6, matrix products, refresh(): jnp.einsum('...mn,...mk->...nk', own_cols, near, preferred_element_type=F32)  11.9 us
  transfers between devices with their start and end apart: 1, of which 0 were waited for; matrix products, arithmetic and copies ran while one was open for 12% of the time, Pallas kernels for 14%

profile of v2, /device:TPU:0, one launch (start us, length us, event | category | flops | bytes accessed | tf_op | source)
XLA Modules:
  0.0 559.9 jit_solution(442186809496935213)
XLA Ops:
  12.6 14.6 %gather_char.1 = (bf16[8,32,1536]{2,1,0:T(8,128)(2,1)S(1)}, s32[8,3,128]{2,1,0:T(4,128)S(1)}) custom-call(bf16[32,1536]{1,0:T(8,128)(2,1)S(1)} %bitcast_dynamic-update-slice_fusion.refs_0_, s32[8,3,128]{2,1,0:T(4,128)S(1)} %sub.143.refs_1_), custom_call_target="tpu_custom_call" | custom-call | tf_op jit(solution)/shard_map/gather_char/pallas_call | solution.py:527
  35.8 18.3 %char_forward.1 = (bf16[640,512]{1,0:T(8,128)(2,1)S(1)}, bf16[20,512,1536]{2,1,0:T(8,128)(2,1)}, bf16[640,256]{1,0:T(8,128)(2,1)S(1)}, f32[640,256]{1,0:T(8,128)S(1)}) custom-call(s32[20]{0:T(128)S(1)} %get-tuple-element.371.kind, bf16[20,512,256]{2,1,0:T(8,128)(2,1)S(1)} %bitcast.500, f32[20,32,128]{2,1,0:T(8,128)S(1)} %broadcast_in_dim.203.count_ref, ...), custom_call_target="tpu_custom_call" | custom-call | flops 10737418240 | bytes 47185920 | tf_op jit(solution)/shard_map/char_forward/pallas_call | solution.py:155
  57.0 23.0 %send_vectors.1 = bf16[8,96,512]{2,1,0:T(8,128)(2,1)S(1)} custom-call(bf16[8,96,512]{2,1,0:T(8,128)(2,1)S(1)} %reshape.836.refs_0_), custom_call_target="tpu_custom_call" | custom-call | tf_op jit(solution)/shard_map/send_vectors/pallas_call | solution.py:527
  80.9 28.1 %gather_words.1 = (bf16[4,320,512]{2,1,0:T(8,128)(2,1)S(1)}, bf16[8,768,128]{2,1,0:T(8,128)(2,1)S(1)}) custom-call(bf16[320,512]{1,0:T(8,128)(2,1)S(1)} %reshape.838.refs_0_, bf16[768,128]{1,0:T(8,128)(2,1)S(1)} %pad_maximum_fusion.4.refs_1_), custom_call_target="tpu_custom_call" | custom-call | tf_op jit(solution)/shard_map/gather_words/pallas_call | solution.py:527
  111.8 2.9 multiply_reduce_fusion.7
  121.8 12.0 %fusion.21 = (pred[512,1024]{1,0:T(8,128)(4,1)S(1)}, pred[512,1024]{1,0:T(8,128)(4,1)S(1)}) fusion(s32[1024]{0:T(1024)S(1)} %bitcast.596, s32[512]{0:T(512)S(1)} %bitcast.599, s32[512]{0:T(512)S(1)} %bitcast.600, s32[512]{0:T(512)S(1)} %iota_add_fusion), kind=kLoop, calls=%fused_computation.56 | loop fusion | flops 3145728 | bytes 1058816 | tf_op jit(solution)/shard_map/while/body/eval_jaxpr/and | solution.py:359
  133.8 3.7 fusion.188
  137.5 3.6 fusion.189
  141.1 3.2 fusion.38
  146.2 50.6 %sum_attend.1 = (bf16[4,256,512]{2,1,0:T(8,128)(2,1)S(1)}, bf16[8,1328,128]{2,1,0:T(8,128)(2,1)S(1)}) custom-call(bf16[4,256,512]{2,1,0:T(8,128)(2,1)S(1)} %bitcast.490, bf16[1328,128]{1,0:T(8,128)(2,1)S(1)} %constant_dynamic-update-slice_fusion.4.refs_1_), custom_call_target="tpu_custom_call" | custom-call | tf_op jit(solution)/shard_map/sum_attend/pallas_call | solution.py:527
  198.4 2.9 copy.248
  217.1 47.9 %sum_part_two.1 = bf16[4,256,512]{2,1,0:T(8,128)(2,1)S(1)} custom-call(bf16[4,256,512]{2,1,0:T(8,128)(2,1)S(1)} %bitcast.494), custom_call_target="tpu_custom_call" | custom-call | tf_op jit(solution)/shard_map/sum_part_two/pallas_call | solution.py:527
  266.7 2.9 copy.257
  269.6 3.5 multiply_reduce_fusion.2
  283.4 3.4 multiply_reduce_fusion
  289.9 4.1 multiply_convert_fusion
  298.4 2.9 fusion.30
  303.9 3.4 fusion.29
  315.1 51.8 %sum_part_one.1 = (bf16[4,256,512]{2,1,0:T(8,128)(2,1)S(1)}, bf16[8,3,64,128]{3,2,1,0:T(8,128)(2,1)S(1)}, bf16[8,16,512]{2,1,0:T(8,128)(2,1)S(1)}, bf16[8,64,512...) custom-call(bf16[4,256,512]{2,1,0:T(8,128)(2,1)S(1)} %bitcast.493, bf16[8,3,64,128]{3,2,1,0:T(8,128)(2,1)S(1)} %bitcast.492, ...), custom_call_target="tpu_custom_call" | custom-call | tf_op jit(solution)/shard_map/sum_part_one/pallas_call | solution.py:527
  371.6 3.3 copy.267
  375.0 3.5 multiply_reduce_fusion.3
  381.7 10.8 %return_vectors.1 = bf16[8,96,512]{2,1,0:T(8,128)(2,1)S(1)} custom-call(bf16[8,96,512]{2,1,0:T(8,128)(2,1)S(1)} %bitcast.495), custom_call_target="tpu_custom_call" | custom-call | tf_op jit(solution)/shard_map/return_vectors/pallas_call | solution.py:527
  404.2 26.1 %char_backward.1 = (bf16[20,512,256]{2,1,0:T(8,128)(2,1)}, f32[256,768]{1,0:T(8,128)S(1)}, f32[256,256]{1,0:T(8,128)S(1)}, f32[256,512]{1,0:T(8,128)S(1)}, f32[1,256]{1,0:T(1,128)S(1)}) custom-call(s32[20]{0:T(128)S(1)} %get-tuple-element.371.kind, bf16[20,512,256]{2,1,0:T(8,128)(2,1)S(1)} %bitcast.501, f32[20,32,128]{2,1,0:T(8,128)S(1)} %copy-done.14, ...), custom_call_target="tpu_custom_call" | custom-call | flops 18790481920 | bytes 47185920 | tf_op jit(solution)/shard_map/char_backward/pallas_call | solution.py:286
  433.6 51.2 %sum_char_grads.1 = (bf16[8,32,1536]{2,1,0:T(8,128)(2,1)S(1)}, f32[8,512]{1,0:T(8,128)S(1)}) custom-call(bf16[8,32,1536]{2,1,0:T(8,128)(2,1)S(1)} %pad_maximum_fusion.2.x, f32[8,512]{1,0:T(8,128)S(1)} %scatter.14.s), custom_call_target="tpu_custom_call" | custom-call | tf_op jit(solution)/shard_map/sum_char_grads/pallas_call | solution.py:602
  (424 shorter events, 159.3 us)
Async XLA Ops:
  7.2 541.6 %all-reduce.3.cloned.1.call-start = ((), (), s32[]{:S(2)}) async-start(), calls=%async_computation | async-start | bytes 2097152 | tf_op jit(solution)/shard_map/psum | solution.py:904
  10.6 45.6 %copy-start.109 = (s32[20]{0:T(128)}, s32[20]{0:T(128)S(1)}, u32[]{:S(2)}) copy-start(s32[20]{0:T(128)S(1)} %get-tuple-element.370) | copy-start | bytes 244
  27.2 26.9 %copy-start.23 = (bf16[8,32,1536]{2,1,0:T(8,128)(2,1)}, bf16[8,32,1536]{2,1,0:T(8,128)(2,1)S(1)}, u32[]{:S(2)}) copy-start(bf16[8,32,1536]{2,1,0:T(8,128)(2,1)S(1)} %get-tuple-element.144) | copy-start | bytes 2359300
  32.3 21.9 %copy-start.17 = (bf16[128,256]{1,0:T(8,128)(2,1)}, bf16[128,256]{1,0:T(8,128)(2,1)S(1)}, u32[]{:S(2)}) copy-start(bf16[128,256]{1,0:T(8,128)(2,1)S(1)} %fusion.121.refs_1_) | copy-start | bytes 196612
  32.5 21.7 %copy-start.15 = (bf16[128,512]{1,0:T(8,128)(2,1)}, bf16[128,512]{1,0:T(8,128)(2,1)S(1)}, u32[]{:S(2)}) copy-start(bf16[128,512]{1,0:T(8,128)(2,1)S(1)} %fusion.108.refs_0_) | copy-start | bytes 393220
  32.6 21.5 %copy-start.13 = (f32[20,32,128]{2,1,0:T(8,128)}, f32[20,32,128]{2,1,0:T(8,128)S(1)}, u32[]{:S(2)}) copy-start(f32[20,32,128]{2,1,0:T(8,128)S(1)} %broadcast_in_dim.203.count_ref) | copy-start | bytes 983044
  80.9 28.3 %copy-start.104 = (f32[2,512]{1,0:T(2,128)S(1)}, f32[2,512]{1,0:T(2,128)}, u32[]{:S(2)}) copy-start(f32[2,512]{1,0:T(2,128)} %param.53) | copy-start | bytes 12292
  116.3 17.5 %copy-start.71 = (bf16[1,512,128]{1,2,0:T(8,128)(2,1)}, bf16[1,512,128]{1,2,0:T(8,128)(2,1)S(1)}, u32[]{:S(2)}) copy-start(bf16[1,512,128]{1,2,0:T(8,128)(2,1)S(1)} %get-tuple-element.343) | copy-start | bytes 393220
  116.3 21.2 %copy-start.72 = (bf16[1,512,128]{1,2,0:T(8,128)(2,1)}, bf16[1,512,128]{1,2,0:T(8,128)(2,1)S(1)}, u32[]{:S(2)}) copy-start(bf16[1,512,128]{1,2,0:T(8,128)(2,1)S(1)} %get-tuple-element.342) | copy-start | bytes 393220
  117.1 20.4 %copy-start.47 = (bf16[1,1024,128]{1,2,0:T(8,128)(2,1)}, bf16[1,1024,128]{1,2,0:T(8,128)(2,1)S(1)}, u32[]{:S(2)}) copy-start(bf16[1,1024,128]{1,2,0:T(8,128)(2,1)S(1)} %get-tuple-element.344) | copy-start | bytes 786436
  492.7 10.6 %copy-start.115 = (f32[1,256]{1,0:T(1,128)}, f32[1,256]{1,0:T(1,128)S(1)}, u32[]{:S(2)}) copy-start(f32[1,256]{1,0:T(1,128)S(1)} %slice_multiply_fusion.2) | copy-start | bytes 3076
  496.2 30.2 %copy-start.40 = (bf16[4,256,256]{2,1,0:T(8,128)(2,1)}, bf16[4,256,256]{2,1,0:T(8,128)(2,1)S(1)}, u32[]{:S(2)}) copy-start(bf16[4,256,256]{2,1,0:T(8,128)(2,1)S(1)} %get-tuple-element.325) | copy-start | bytes 1572868
  498.6 30.8 %copy-start.38 = (bf16[8,64,512]{2,1,0:T(8,128)(2,1)}, bf16[8,64,512]{2,1,0:T(8,128)(2,1)S(1)}, u32[]{:S(2)}) copy-start(bf16[8,64,512]{2,1,0:T(8,128)(2,1)S(1)} %get-tuple-element.346) | copy-start | bytes 1572868
  507.8 11.4 %copy-start.99 = (f32[1,32,256]{2,1,0:T(8,128)S(1)}, f32[1,32,256]{2,1,0:T(8,128)}, u32[]{:S(2)}) copy-start(f32[1,32,256]{2,1,0:T(8,128)} %param.60) | copy-start | bytes 98308
  507.8 13.1 %copy-start.59 = (bf16[8,16,512]{2,1,0:T(8,128)(2,1)S(1)}, bf16[8,16,512]{2,1,0:T(8,128)(2,1)}, u32[]{:S(2)}) copy-start(bf16[8,16,512]{2,1,0:T(8,128)(2,1)} %get-tuple-element.354) | copy-start | bytes 393220
  507.8 15.0 %copy-start.58 = (bf16[8,1,4,64,128]{4,2,3,0,1:T(4,128)(2,1)S(1)}, bf16[8,1,4,64,128]{4,2,3,0,1:T(4,128)(2,1)}, u32[]{:S(2)}) copy-start(bf16[8,1,4,64,128]{4,2,3,0,1:T(4,128)(2,1)} %copy.281) | copy-start | bytes 1572868
  507.8 15.0 %copy-start.86 = (f32[1,16,512]{2,1,0:T(8,128)S(1)}, f32[1,16,512]{2,1,0:T(8,128)}, u32[]{:S(2)}) copy-start(f32[1,16,512]{2,1,0:T(8,128)} %param.69) | copy-start | bytes 98308
  507.9 15.0 %copy-start.108 = (f32[1,16,128]{2,1,0:T(8,128)S(1)}, f32[1,16,128]{2,1,0:T(8,128)}, u32[]{:S(2)}) copy-start(f32[1,16,128]{2,1,0:T(8,128)} %param.72) | copy-start | bytes 24580
  508.7 15.0 %copy-start.94 = (f32[1,16,512]{2,1,0:T(8,128)}, f32[1,16,512]{2,1,0:T(8,128)S(1)}, u32[]{:S(2)}) copy-start(f32[1,16,512]{2,1,0:T(8,128)S(1)} %constant_dynamic-slice_fusion.2) | copy-start | bytes 98308
  510.9 12.8 %copy-start.110 = (f32[1,16,128]{2,1,0:T(8,128)S(1)}, f32[1,16,128]{2,1,0:T(8,128)}, u32[]{:S(2)}) copy-start(f32[1,16,128]{2,1,0:T(8,128)} %param.70) | copy-start | bytes 24580
  513.4 16.0 %copy-start.67 = (f32[1,64,512]{2,1,0:T(8,128)}, f32[1,64,512]{2,1,0:T(8,128)S(1)}, u32[]{:S(2)}) copy-start(f32[1,64,512]{2,1,0:T(8,128)S(1)} %constant_dynamic-slice_fusion) | copy-start | bytes 393220
  514.4 18.0 %copy-start.68 = (f32[1,64,512]{2,1,0:T(8,128)}, f32[1,64,512]{2,1,0:T(8,128)S(1)}, u32[]{:S(2)}) copy-start(f32[1,64,512]{2,1,0:T(8,128)S(1)} %constant_dynamic-slice_fusion.1) | copy-start | bytes 393220
  514.4 12.1 %copy-start.82 = (f32[4,32,256]{2,1,0:T(8,128)S(1)}, f32[4,32,256]{2,1,0:T(8,128)}, u32[]{:S(2)}) copy-start(f32[4,32,256]{2,1,0:T(8,128)} %param.55) | copy-start | bytes 393220
  519.2 10.2 %copy-start.69 = (f32[4,32,256]{2,1,0:T(8,128)}, f32[4,32,256]{2,1,0:T(8,128)S(1)}, u32[]{:S(2)}) copy-start(f32[4,32,256]{2,1,0:T(8,128)S(1)} %constant_dynamic-slice_fusion.3) | copy-start | bytes 393220
  (93 other events, 300.6 us)
Sparse Core Ops, SparseCore 0:
  396.7 55.9 all-reduce.2
